TPU v7x, 512 devices: a whole 4x8x8 slice. The times are simulated.
512 devices in a mesh: tenant: 16 (over y_hi, z), feat: 32 (over y_lo, x, core).
Axes of the slice: x: 4, y: 8 (y_hi: 2, y_lo: 4; y = y_hi * 4 + y_lo), z: 8, core: 2. Of those that a mesh axis runs over, the one named last changes fastest.
Arguments:
- adapter_input_weight: float32 [512, 16, 8192], P('tenant', None, 'feat'), may hold values from -3 to 3
- adapter_output_weight: float32 [512, 16, 8192], P('tenant', None, 'feat'), may hold values from -3 to 3
- initial_output_basis: float32 [8192, 256], P('feat'), may hold values from -6 to 6
- initial_input_basis: float32 [8192, 256], P('feat'), may hold values from -6 to 6
Outputs:
- cores: float32 [512, 256, 256], P('tenant', 'feat')
- output_basis: float32 [8192, 256], P('feat')
- input_basis: float32 [8192, 256], P('feat')
All inputs are finite; a program needn't handle non-finite values.
Results may differ from a plain program's by a relative error of at most 0.0003.
Values sent between devices are 32-bit elements; how exact they have to be, the bound alone decides.
No kernel may reach another device: no remote copies, remote signals or barrier semaphores. Data moves between devices by JAX's collectives and lax.ppermute only.
A program may use at most 64 MiB of HBM per device.

v0:
```python
import math

import jax
import jax.numpy as jnp
from jax import lax
from jax.sharding import PartitionSpec as P

PROJ_WIDTH = 8192
ITERS = 2


HIGH_PRECISION = lax.Precision.HIGHEST


def project_locally(shared_basis, adapter_weights):
    return jnp.einsum(
        "pyw,wj->pyj", adapter_weights, shared_basis, precision=HIGH_PRECISION
    ) / math.sqrt(PROJ_WIDTH)


def gram_of(raw_basis):
    return jnp.dot(raw_basis.T, raw_basis, precision=HIGH_PRECISION)


def apply_factor(raw_basis, gram_matrix):
    lower_factor = jnp.linalg.cholesky(gram_matrix / PROJ_WIDTH)
    return jax.scipy.linalg.solve_triangular(lower_factor, raw_basis.T, lower=True).T


def tenant_grams(proj_x):
    return jnp.einsum("trk,tsk->trs", proj_x, proj_x, precision=HIGH_PRECISION)


def body(adapter_input_weight, adapter_output_weight, initial_output_basis, initial_input_basis):
    output_basis, input_basis = (initial_output_basis, initial_input_basis)
    cores = None
    for step in range(ITERS + 1):
        final_round = step == ITERS
        partial_output_sum = project_locally(output_basis, adapter_output_weight)
        partial_input_sum = project_locally(input_basis, adapter_input_weight)
        projected_output, projected_input = lax.psum(
            (partial_output_sum, partial_input_sum), "feat"
        )
        if final_round:
            row_count = projected_output.shape[2] // lax.axis_size("feat")
            offset = lax.axis_index("feat") * row_count
            my_cols = lax.dynamic_slice_in_dim(projected_output, offset, row_count, 2)
            cores = jnp.einsum("trk,trl->tkl", my_cols, projected_input, precision=HIGH_PRECISION)
        else:
            output_factor = jnp.einsum(
                "trs,tsk->trk",
                tenant_grams(projected_input),
                projected_output,
                precision=HIGH_PRECISION,
            )
            input_factor = jnp.einsum(
                "trs,tsk->trk",
                tenant_grams(projected_output),
                projected_input,
                precision=HIGH_PRECISION,
            )
        if not final_round:
            updated_output_basis = jnp.einsum(
                "hos,hol->sl", adapter_output_weight, output_factor, precision=HIGH_PRECISION
            )
            updated_input_basis = jnp.einsum(
                "hos,hol->sl", adapter_input_weight, input_factor, precision=HIGH_PRECISION
            )
            updated_output_basis, updated_input_basis = lax.psum(
                (updated_output_basis, updated_input_basis), "tenant"
            )
            gram_u, gram_v = lax.psum(
                (gram_of(updated_output_basis), gram_of(updated_input_basis)), "feat"
            )
            output_basis = apply_factor(updated_output_basis, gram_u)
            input_basis = apply_factor(updated_input_basis, gram_v)
    return (cores, output_basis, input_basis)


def solution(mesh):
    placed = (
        P("tenant", None, "feat"),
        P("tenant", None, "feat"),
        P("feat", None),
        P("feat", None),
    )
    return jax.shard_map(
        body,
        mesh=mesh,
        in_specs=placed,
        out_specs=(P("tenant", "feat", None), P("feat", None), P("feat", None)),
        check_vma=False,
    )
```

profile of v0, /device:TPU:1, one launch (start us, length us, event | category | flops | bytes accessed | tf_op | source)
XLA Modules:
  0.0 2107.2 jit_solution(8441556930042441545)
XLA Ops:
  7.2 2.6 convolution_multiply_fusion.4
  9.8 1.4 convolution_multiply_fusion.5
  11.2 289.2 %all-reduce.24.cloned.1.call-done = (f32[32,16,256]{2,1,0:T(8,128)}, f32[32,16,256]{2,1,0:T(8,128)}) async-done(((f32[32,16,256]{2,1,0:T(8,128)}, f32[32,16,256]{2,1,0:T(8,128)}), (f32[32,16,256]{2,1,0:T(8,128)}, f32[32,16,256]{2,1,0:T(8,128)})) %all-reduce.24.cloned.1.call-update) | async-done | bytes 1048592 | tf_op jit(solution)/shard_map/psum | solution.py:41
  300.4 1.9 fusion.77
  303.9 1.7 convolution_bitcast_fusion.3
  306.3 1.7 convolution_bitcast_fusion.2
  308.1 185.8 %all-reduce.28.cloned.1.call-done = (f32[256,256]{0,1:T(8,128)}, f32[256,256]{0,1:T(8,128)}) async-done(((f32[256,256]{0,1:T(8,128)}, f32[256,256]{0,1:T(8,128)}), (f32[256,256]{0,1:T(8,128)}, f32[256,256]{0,1:T(8,128)})) %all-reduce.28.cloned.1.call-update) | async-done | bytes 524304 | tf_op jit(solution)/shard_map/psum | solution.py:69
  493.9 2.2 fusion.79
  496.1 1.1 fusion.82
  497.5 289.2 %all-reduce.22.cloned.1.call-done = (f32[256,256]{0,1:T(8,128)}, f32[256,256]{0,1:T(8,128)}) async-done(((f32[256,256]{0,1:T(8,128)}, f32[256,256]{0,1:T(8,128)}), (f32[256,256]{0,1:T(8,128)}, f32[256,256]{0,1:T(8,128)})) %all-reduce.22.cloned.1.call-update) | async-done | bytes 524304 | tf_op jit(solution)/shard_map/psum | solution.py:72
  786.6 1.0 broadcast_multiply_fusion.2
  787.7 0.8 copy-done.13
  788.7 0.8 copy-done.12
  789.6 11.7 cholesky.214
  801.4 9.8 custom-call.17
  811.7 11.7 cholesky.231
  826.1 4.0 while.8
  826.7 1.4 bitcast_dynamic-update-slice_fusion.8
  828.8 1.4 bitcast_dynamic-update-slice_fusion.8
  830.1 19.9 custom-call.18
  851.0 1.6 fusion.3
  852.6 11.7 cholesky.248
  864.3 9.8 custom-call.19
  874.6 11.7 cholesky.265
  886.4 0.6 compare_reduce_fusion.4
  889.0 4.0 while.9
  889.6 1.4 bitcast_dynamic-update-slice_fusion.9
  891.6 1.4 bitcast_dynamic-update-slice_fusion.9
  893.0 20.1 custom-call.20
  914.0 1.6 fusion.2
  915.7 282.7 %all-reduce.20.cloned.1.call-done = (f32[32,16,256]{2,0,1:T(8,128)}, f32[32,16,256]{2,0,1:T(8,128)}) async-done(((f32[32,16,256]{2,0,1:T(8,128)}, f32[32,16,256]{2,0,1:T(8,128)}), (f32[32,16,256]{2,0,1:T(8,128)}, f32[32,16,256]{2,0,1:T(8,128)})) %all-reduce.20.cloned.1.call-update) | async-done | bytes 1048592 | tf_op jit(solution)/shard_map/psum | solution.py:41
  1198.4 2.4 fusion.12
  1200.9 0.9 fusion.6
  1201.7 0.8 fusion.8
  1202.6 1.7 convolution_bitcast_fusion.1
  1204.3 0.8 fusion.10
  1205.2 1.7 convolution_bitcast_fusion
  1207.0 185.8 %all-reduce.26.cloned.1.call-done = (f32[256,256]{0,1:T(8,128)}, f32[256,256]{0,1:T(8,128)}) async-done(((f32[256,256]{0,1:T(8,128)}, f32[256,256]{0,1:T(8,128)}), (f32[256,256]{0,1:T(8,128)}, f32[256,256]{0,1:T(8,128)})) %all-reduce.26.cloned.1.call-update) | async-done | bytes 524304 | tf_op jit(solution)/shard_map/psum | solution.py:69
  1392.8 2.2 fusion.83
  1395.0 1.1 fusion.84
  1396.4 289.3 %all-reduce.18.cloned.1.call-done = (f32[256,256]{0,1:T(8,128)}, f32[256,256]{0,1:T(8,128)}) async-done(((f32[256,256]{0,1:T(8,128)}, f32[256,256]{0,1:T(8,128)}), (f32[256,256]{0,1:T(8,128)}, f32[256,256]{0,1:T(8,128)})) %all-reduce.18.cloned.1.call-update) | async-done | bytes 524304 | tf_op jit(solution)/shard_map/psum | solution.py:72
  1685.7 1.0 broadcast_multiply_fusion
  1686.8 0.8 copy-done.11
  1687.7 11.7 cholesky.316
  1699.4 9.8 custom-call.23
  1709.7 11.7 cholesky.333
  1724.1 4.0 while.11
  1724.7 1.4 bitcast_dynamic-update-slice_fusion.11
  1726.7 1.4 bitcast_dynamic-update-slice_fusion.11
  1728.1 19.9 custom-call.24
  1749.8 11.7 cholesky.282
  1761.5 9.8 custom-call.21
  1771.8 11.7 cholesky.299
  1786.2 4.0 while.10
  1786.8 1.4 bitcast_dynamic-update-slice_fusion.10
  1788.8 1.4 bitcast_dynamic-update-slice_fusion.10
  1790.2 19.9 custom-call.22
  1811.1 1.6 fusion.1
  1812.7 1.6 fusion
  1814.4 0.8 copy.24
  1815.2 0.8 copy.23
  1816.1 281.0 %all-reduce.16.cloned.1.call-done = (f32[32,16,256]{2,0,1:T(8,128)}, f32[32,16,256]{2,0,1:T(8,128)}) async-done(((f32[32,16,256]{2,0,1:T(8,128)}, f32[32,16,256]{2,0,1:T(8,128)}), (f32[32,16,256]{2,0,1:T(8,128)}, f32[32,16,256]{2,0,1:T(8,128)})) %all-reduce.16.cloned.1.call-update) | async-done | bytes 1048592 | tf_op jit(solution)/shard_map/psum | solution.py:41
  2097.1 1.1 constant_dynamic-slice_fusion.4
  2098.2 1.7 fusion.4
  (126 shorter events, 19.5 us)
Async XLA Ops:
  7.2 2.6 copy-start
  7.2 2.6 copy-start.15
  7.2 293.2 %all-reduce.24.cloned.1.call-start = ((), (), s32[]{:S(2)}) async-start(), calls=%async_computation.4 | async-start | bytes 2097152 | tf_op jit(solution)/shard_map/psum | solution.py:41
  11.2 482.7 %all-reduce.28.cloned.1.call-start = ((), (), s32[]{:S(2)}) async-start(), calls=%async_computation.6 | async-start | bytes 1048576 | tf_op jit(solution)/shard_map/psum | solution.py:69
  300.4 1.9 copy-start.2
  302.9 1.0 copy-start.3
  303.9 1.7 copy-start.1
  308.0 478.6 %all-reduce.22.cloned.1.call-start = ((), (), s32[]{:S(2)}) async-start(), calls=%async_computation.3 | async-start | bytes 1048576 | tf_op jit(solution)/shard_map/psum | solution.py:72
  493.9 2.2 copy-start.4
  497.2 701.2 %all-reduce.20.cloned.1.call-start = ((), (), s32[]{:S(2)}) async-start(), calls=%async_computation.2 | async-start | bytes 2097152 | tf_op jit(solution)/shard_map/psum | solution.py:41
  787.6 1.0 copy-start.13
  788.6 1.0 copy-start.12
  826.1 23.9 %copy-start.6 = (f32[256,256]{0,1:T(8,128)S(1)}, f32[256,256]{0,1:T(8,128)}, u32[]{:S(2)}) copy-start(f32[256,256]{0,1:T(8,128)} %get-tuple-element.83) | copy-start | bytes 786436
  915.7 477.1 %all-reduce.26.cloned.1.call-start = ((), (), s32[]{:S(2)}) async-start(), calls=%async_computation.5 | async-start | bytes 1048576 | tf_op jit(solution)/shard_map/psum | solution.py:69
  1198.4 2.4 copy-start.9
  1202.6 1.7 copy-start.8
  1206.9 478.8 %all-reduce.18.cloned.1.call-start = ((), (), s32[]{:S(2)}) async-start(), calls=%async_computation.1 | async-start | bytes 1048576 | tf_op jit(solution)/shard_map/psum | solution.py:72
  1392.8 2.2 copy-start.7
  1396.2 700.9 %all-reduce.16.cloned.1.call-start = ((), (), s32[]{:S(2)}) async-start(), calls=%async_computation | async-start | bytes 2097152 | tf_op jit(solution)/shard_map/psum | solution.py:41
  1686.7 1.0 copy-start.11
  1748.6 1.0 copy-start.10
  1786.2 24.0 %copy-start.5 = (f32[256,256]{0,1:T(8,128)S(1)}, f32[256,256]{0,1:T(8,128)}, u32[]{:S(2)}) copy-start(f32[256,256]{0,1:T(8,128)} %get-tuple-element.81) | copy-start | bytes 786436
  2097.1 1.1 copy-start.14
Sparse Core Ops, SparseCore 0:
  11.3 289.0 all-reduce.23
  308.1 185.7 all-reduce.27
  497.4 289.1 all-reduce.21
  915.8 282.5 all-reduce.19
  1207.0 185.7 all-reduce.25
  1396.5 289.1 all-reduce.17
  1814.4 282.5 all-reduce.15
where the time goes:
time: 2110 us
  waiting for transfers between devices  1800 us (85%)
  other arithmetic  220 us (10%)
  matrix products  39.6 us (2%)
  local copies, waits for them, and re-layouts  22.9 us (1%)
    psum x3, waiting for transfers between devices, body(): lax.psum((partial_output_sum, partial_input_sum), 'feat')  853 us
    psum x2, waiting for transfers between devices, body(): lax.psum((gram_of(updated_output_basis), gram_of(updated_input_basis)), '...  578 us
    psum x2, waiting for transfers between devices, body(): lax.psum((updated_output_basis, updated_input_basis), 'tenant')  372 us
    another operation x28, other arithmetic, apply_factor(): lower_factor = jnp.linalg.cholesky(gram_matrix / PROJ_WIDTH)  138 us
    another operation x9, other arithmetic, apply_factor(): jax.scipy.linalg.solve_triangular(lower_factor, raw_basis.T, lower=True)  79.9 us
  transfers between devices with their start and end apart: 7, of which 7 were waited for; matrix products, arithmetic and copies ran while one was open for 0% of the time, Pallas kernels for 0%

commit v1 on v0

v1 whole, which is shorter than its diff:
```python
import math

import jax
import jax.numpy as jnp
from jax import lax
from jax.sharding import PartitionSpec as P

PROJ_WIDTH = 8192
ITERS = 2
HIGH_PRECISION = lax.Precision.HIGHEST


def mm(a, b, ca, cb):
    return lax.dot_general(
        a, b, (((ca,), (cb,)), ((), ())), precision=HIGH_PRECISION,
        preferred_element_type=jnp.float32,
    )


def bmm(a, b, ca, cb):
    return lax.dot_general(
        a, b, (((ca,), (cb,)), ((0,), (0,))), precision=HIGH_PRECISION,
        preferred_element_type=jnp.float32,
    )


def scatter_sum(chunks, axis):
    return jnp.sum(lax.all_to_all(chunks, axis, 0, 0, tiled=True), axis=0)


def gather(own, axis):
    n = lax.axis_size(axis)
    return lax.all_to_all(
        jnp.broadcast_to(own[None], (n,) + own.shape), axis, 0, 0, tiled=True
    )


def inverse_factor(gram_matrix):
    lower_factor = jnp.linalg.cholesky(gram_matrix / PROJ_WIDTH)
    return jax.scipy.linalg.solve_triangular(
        lower_factor, jnp.eye(gram_matrix.shape[0], dtype=jnp.float32), lower=True
    )


def update(w_out, w_in, factor_out, factor_in):
    parts = jnp.stack([mm(w_out, factor_out, 0, 0), mm(w_in, factor_in, 0, 0)])
    n = lax.axis_size("tenant")
    two, feats, r = parts.shape
    chunks = parts.reshape(2, n, feats // n, r).transpose(1, 0, 2, 3)
    whole = gather(scatter_sum(chunks, "tenant"), "tenant")
    whole = whole.transpose(1, 0, 2, 3).reshape(2, feats, r)
    return whole[0], whole[1]


def body(adapter_input_weight, adapter_output_weight, initial_output_basis, initial_input_basis):
    tenants, rank, feats = adapter_output_weight.shape
    r = initial_output_basis.shape[1]
    n = lax.axis_size("feat")
    w_out = adapter_output_weight.reshape(tenants * rank, feats)
    w_in = adapter_input_weight.reshape(tenants * rank, feats)
    root = 1.0 / math.sqrt(PROJ_WIDTH)

    def projections(u, v):
        return [
            mm(w_out, u, 1, 0).reshape(n, rank, r),
            mm(w_in, v, 1, 0).reshape(n, rank, r),
        ]

    own = scatter_sum(jnp.concatenate(projections(initial_output_basis, initial_input_basis), 1), "feat")
    own = own * root
    p, q = own[:rank], own[rank:]
    f_out = mm(mm(q, q, 1, 1), p, 1, 0)
    f_in = mm(mm(p, p, 1, 1), q, 1, 0)
    factors = gather(jnp.concatenate([f_out, f_in], 0), "feat")
    f_out = factors[:, :rank].reshape(tenants * rank, r)
    f_in = factors[:, rank:].reshape(tenants * rank, r)

    for step in range(ITERS):
        u_new, v_new = update(w_out, w_in, f_out, f_in)
        grams = [
            mm(u_new, u_new, 0, 0).reshape(n, r // n, r),
            mm(v_new, v_new, 0, 0).reshape(n, r // n, r),
        ]
        own = scatter_sum(jnp.concatenate(projections(u_new, v_new) + grams, 1), "feat")
        last = step == ITERS - 1
        whole = gather(own[2 * rank:] if last else own, "feat")
        grams = whole if last else whole[:, 2 * rank:]
        half = r // n
        x_out = inverse_factor(grams[:, :half].reshape(r, r))
        x_in = inverse_factor(grams[:, half:].reshape(r, r))
        if not last:
            p = mm(whole[:, :rank].reshape(tenants * rank, r), x_out, 1, 1) * root
            q = mm(whole[:, rank:2 * rank].reshape(tenants * rank, r), x_in, 1, 1) * root
            p = p.reshape(tenants, rank, r)
            q = q.reshape(tenants, rank, r)
            f_out = bmm(bmm(q, q, 2, 2), p, 2, 1).reshape(tenants * rank, r)
            f_in = bmm(bmm(p, p, 2, 2), q, 2, 1).reshape(tenants * rank, r)
        else:
            p = mm(own[:rank], x_out, 1, 1) * root
            q = mm(own[rank:2 * rank], x_in, 1, 1) * root
            core = mm(p, q, 0, 0).reshape(n, r // n, r)
            cores = lax.all_to_all(core, "feat", 0, 0, tiled=True)
            u = mm(u_new, x_out, 1, 1)
            v = mm(v_new, x_in, 1, 1)
    return (cores, u, v)


def solution(mesh):
    placed = (
        P("tenant", None, "feat"),
        P("tenant", None, "feat"),
        P("feat", None),
        P("feat", None),
    )
    return jax.shard_map(
        body,
        mesh=mesh,
        in_specs=placed,
        out_specs=(P("tenant", "feat", None), P("feat", None), P("feat", None)),
        check_vma=False,
    )
```

time: 2110 us -> 627 us (0.30)
  waiting for transfers between devices: 1800 us -> 88.7 us
  blocking collectives: 0 us -> 225 us
  starting transfers between devices: 0.63 us -> 23.5 us
    psum x7 -> x0, waiting for transfers between devices: 1800 us -> none  [the longest x3 853 us: body(): lax.psum((partial_output_sum, partial_input_sum), 'feat')]
    all_to_all x0 -> x7, blocking collectives: none -> 225 us  [the longest x4 145 us: scatter_sum(): return jnp.sum(lax.all_to_all(chunks, axis, 0, 0, tiled=True), axis=0)]
    all_to_all x0 -> x4, waiting for transfers between devices: none -> 88.7 us  [the longest x2 53.1 us: gather(): lax.all_to_all(jnp.broadcast_to(own[None], (n,) + own.shape), axis, 0, 0,...]
    all_to_all x0 -> x4, starting transfers between devices: none -> 23.5 us  [the longest x1 10.5 us: scatter_sum(): return jnp.sum(lax.all_to_all(chunks, axis, 0, 0, tiled=True), axis=0)]
    another operation x37 -> x35, other arithmetic: 218 us -> 217 us  [the longest x26 137 us: inverse_factor(): lower_factor = jnp.linalg.cholesky(gram_matrix / PROJ_WIDTH)]
  transfers between devices with their start and end apart: 7 -> 4, of which waited for: 7 -> 4; matrix products, arithmetic and copies ran while one was open for 0% -> 0% of each run, Pallas kernels for 0% -> 0%
where the time goes in v1:
time: 627 us; the launch traced here: 618 us
  blocking collectives  225 us (36%)
  other arithmetic  220 us (35%)
  waiting for transfers between devices  88.7 us (14%)
  matrix products  30 us (5%)
  local copies, waits for them, and re-layouts  23.7 us (4%)
  starting transfers between devices  23.5 us (4%)
  between operations  6.94 us (1%)
    all_to_all x4, blocking collectives, scatter_sum(): return jnp.sum(lax.all_to_all(chunks, axis, 0, 0, tiled=True), axis=0)  145 us
    another operation x26, other arithmetic, inverse_factor(): lower_factor = jnp.linalg.cholesky(gram_matrix / PROJ_WIDTH)  137 us
    all_to_all x3, blocking collectives, gather(): lax.all_to_all(jnp.broadcast_to(own[None], (n,) + own.shape), axis, 0, 0,...  80 us
    another operation x9, other arithmetic, inverse_factor(): jax.scipy.linalg.solve_triangular(lower_factor, jnp.eye(gram_matrix.shape...  79.6 us
    all_to_all x2, waiting for transfers between devices, gather(): lax.all_to_all(jnp.broadcast_to(own[None], (n,) + own.shape), axis, 0, 0,...  53.1 us
    all_to_all x1, waiting for transfers between devices, scatter_sum(): return jnp.sum(lax.all_to_all(chunks, axis, 0, 0, tiled=True), axis=0)  26.7 us
    dot_general x25, matrix products, mm(): lax.dot_general(a, b, (((ca,), (cb,)), ((), ())), precision=HIGH_PRECISIO...  20.6 us
    another operation x29, local copies, waits for them, and re-layouts, inverse_factor(): jax.scipy.linalg.solve_triangular(lower_factor, jnp.eye(gram_matrix.shape...  16.1 us
  transfers between devices with their start and end apart: 4, of which 4 were waited for; matrix products, arithmetic and copies ran while one was open for 0% of the time, Pallas kernels for 0%

profile of v1, /device:TPU:1, one launch (start us, length us, event | category | flops | bytes accessed | tf_op | source)
XLA Modules:
  0.0 617.9 jit_solution(5941163315523396345)
XLA Ops:
  0.6 1.7 fusion.28
  2.4 1.5 fusion.30
  3.9 1.1 pad_maximum_fusion.2
  5.0 10.5 %all-to-all-start = ((f32[32,32,256]{2,1,0:T(8,128)}), f32[32,32,256]{2,1,0:T(8,128)S(1)}, u32[]{:S(2)}, u32[]{:S(2)}) async-start(f32[32,32,256]{2,1,0:T(8,128)} %pad_maximum_fusion.2), calls=%async_computation | async-start | bytes 2097152 | tf_op jit(solution)/shard_map/all_to_all | solution.py:28
  15.5 26.7 %all-to-all-done = f32[32,32,256]{2,1,0:T(8,128)S(1)} async-done(((f32[32,32,256]{2,1,0:T(8,128)}), f32[32,32,256]{2,1,0:T(8,128)S(1)}, u32[]{:S(2)}, u32[]{:S(2)}) %all-to-all-start) | async-done | bytes 1048608 | tf_op jit(solution)/shard_map/all_to_all | solution.py:28
  43.0 31.5 %all_to_all.55 = f32[32,32,256]{2,1,0:T(8,128)S(1)} all-to-all(f32[32,32,256]{2,1,0:T(8,128)S(1)} %broadcast_in_dim.10), channel_id=1, replica_groups=mesh['tenant'=16,'feat'=32] {'feat'}, dimensions={0} | all-to-all | bytes 2097152 | tf_op jit(solution)/shard_map/all_to_all | solution.py:33
  74.6 1.5 fusion.2
  76.0 1.5 fusion
  77.6 26.8 %all_to_all.58 = f32[16,2,16,256]{3,2,1,0:T(8,128)S(1)} all-to-all(f32[16,2,16,256]{3,2,1,0:T(8,128)S(1)} %maximum_bitcast_fusion), channel_id=1, replica_groups=mesh['tenant'=16,'feat'=32] {'tenant'}, dimensions={0} | all-to-all | bytes 1048576 | tf_op jit(solution)/shard_map/all_to_all | solution.py:28
  104.4 23.8 %all_to_all.56 = f32[16,2,16,256]{3,2,1,0:T(8,128)S(1)} all-to-all(f32[16,2,16,256]{3,2,1,0:T(8,128)S(1)} %broadcast_in_dim.11), channel_id=1, replica_groups=mesh['tenant'=16,'feat'=32] {'tenant'}, dimensions={0} | all-to-all | bytes 1048576 | tf_op jit(solution)/shard_map/all_to_all | solution.py:33
  128.2 0.8 copy.47
  129.2 1.0 convolution_bitcast_fusion.3
  130.5 1.0 convolution_bitcast_fusion.2
  131.7 1.3 fusion.26
  133.6 48.7 %all_to_all.59 = f32[32,48,256]{2,1,0:T(8,128)S(1)} all-to-all(f32[32,48,256]{2,1,0:T(8,128)S(1)} %pad_maximum_fusion), channel_id=1, replica_groups=mesh['tenant'=16,'feat'=32] {'feat'}, dimensions={0} | all-to-all | bytes 3145728 | tf_op jit(solution)/shard_map/all_to_all | solution.py:28
  182.3 1.3 broadcast_in_dim.12
  183.7 4.7 all-to-all-start.5
  188.5 36.7 %all-to-all-done.5 = f32[32,48,256]{2,1,0:T(8,128)S(1)} async-done(((f32[32,48,256]{2,1,0:T(8,128)}), f32[32,48,256]{2,1,0:T(8,128)S(1)}, u32[]{:S(2)}, u32[]{:S(2)}) %all-to-all-start.5) | async-done | bytes 1572896 | tf_op jit(solution)/shard_map/all_to_all | solution.py:33
  226.1 1.1 copy.50
  228.6 11.7 %cholesky.214 = f32[128,128]{1,0:T(8,128)S(1)} custom-call(f32[128,128]{1,0:T(8,128)S(1)} %cholesky.346), custom_call_target="Cholesky" | custom-call | tf_op jit(solution)/shard_map/jit(cholesky)/cholesky | solution.py:39
  240.4 9.8 %custom-call.17 = f32[1,128,128]{1,2,0:T(8,128)S(1)} custom-call(f32[1,128,128]{2,1,0:T(8,128)S(1)} %get-tuple-element.102), custom_call_target="InvertDiagBlocksLowerTriangular" | custom-call | tf_op jit(solution)/shard_map/jit(cholesky)/cholesky | solution.py:39
  250.2 1.0 constant_dynamic-update-slice_fusion.7
  251.3 1.1 convolution_subtract_fusion.7
  252.4 11.7 %cholesky.231 = f32[128,128]{1,0:T(8,128)S(1)} custom-call(f32[128,128]{1,0:T(8,128)S(1)} %convolution_subtract_fusion.7), custom_call_target="Cholesky" | custom-call | tf_op jit(solution)/shard_map/jit(cholesky)/cholesky | solution.py:39
  266.3 4.1 while.8
  267.0 1.4 bitcast_dynamic-update-slice_fusion.8
  269.0 1.4 bitcast_dynamic-update-slice_fusion.8
  270.5 19.8 %custom-call.18 = f32[2,128,128]{1,2,0:T(8,128)S(1)} custom-call(f32[2,128,128]{2,1,0:T(8,128)S(1)} %get-tuple-element.31), custom_call_target="InvertDiagBlocksLowerTriangular" | custom-call | tf_op jit(solution)/shard_map/jit(_solve_triangular)/triangular_solve | solution.py:40
  292.6 11.7 %cholesky.248 = f32[128,128]{1,0:T(8,128)S(1)} custom-call(f32[128,128]{1,0:T(8,128)S(1)} %cholesky.349), custom_call_target="Cholesky" | custom-call | tf_op jit(solution)/shard_map/jit(cholesky)/cholesky | solution.py:39
  304.3 9.8 %custom-call.19 = f32[1,128,128]{1,2,0:T(8,128)S(1)} custom-call(f32[1,128,128]{2,1,0:T(8,128)S(1)} %get-tuple-element.106), custom_call_target="InvertDiagBlocksLowerTriangular" | custom-call | tf_op jit(solution)/shard_map/jit(cholesky)/cholesky | solution.py:39
  314.6 11.7 %cholesky.265 = f32[128,128]{1,0:T(8,128)S(1)} custom-call(f32[128,128]{1,0:T(8,128)S(1)} %convolution_subtract_fusion.6), custom_call_target="Cholesky" | custom-call | tf_op jit(solution)/shard_map/jit(cholesky)/cholesky | solution.py:39
  328.6 4.0 while.9
  329.2 1.4 bitcast_dynamic-update-slice_fusion.9
  331.2 1.4 bitcast_dynamic-update-slice_fusion.9
  332.6 19.7 %custom-call.20 = f32[2,128,128]{1,2,0:T(8,128)S(1)} custom-call(f32[2,128,128]{2,1,0:T(8,128)S(1)} %get-tuple-element.32), custom_call_target="InvertDiagBlocksLowerTriangular" | custom-call | tf_op jit(solution)/shard_map/jit(_solve_triangular)/triangular_solve | solution.py:40
  355.0 1.0 fusion.89
  356.6 1.0 fusion.92
  357.6 19.2 %all_to_all.60 = f32[16,2,16,256]{3,2,1,0:T(8,128)S(1)} all-to-all(f32[16,2,16,256]{3,2,1,0:T(8,128)S(1)} %maximum_bitcast_fusion.1), channel_id=1, replica_groups=mesh['tenant'=16,'feat'=32] {'tenant'}, dimensions={0} | all-to-all | bytes 1048576 | tf_op jit(solution)/shard_map/all_to_all | solution.py:28
  376.9 24.7 %all_to_all.57 = f32[16,2,16,256]{3,2,1,0:T(8,128)S(1)} all-to-all(f32[16,2,16,256]{3,2,1,0:T(8,128)S(1)} %broadcast_in_dim.14), channel_id=1, replica_groups=mesh['tenant'=16,'feat'=32] {'tenant'}, dimensions={0} | all-to-all | bytes 1048576 | tf_op jit(solution)/shard_map/all_to_all | solution.py:33
  401.7 1.0 convolution_bitcast_fusion.1
  402.9 1.0 convolution_bitcast_fusion
  405.4 49.9 %all_to_all.61 = f32[32,48,256]{2,1,0:T(8,128)S(1)} all-to-all(f32[32,48,256]{2,1,0:T(8,128)S(1)} %pad_maximum_fusion.1), channel_id=1, replica_groups=mesh['tenant'=16,'feat'=32] {'feat'}, dimensions={0} | all-to-all | bytes 3145728 | tf_op jit(solution)/shard_map/all_to_all | solution.py:28
  455.4 0.8 broadcast_in_dim.15
  456.2 4.2 all-to-all-start.9
  460.4 16.4 %all-to-all-done.9 = f32[32,16,256]{2,1,0:T(8,128)S(1)} async-done(((f32[32,16,256]{2,1,0:T(8,128)}), f32[32,16,256]{2,1,0:T(8,128)S(1)}, u32[]{:S(2)}, u32[]{:S(2)}) %all-to-all-start.9) | async-done | bytes 524320 | tf_op jit(solution)/shard_map/all_to_all | solution.py:33
  477.2 11.7 %cholesky.316 = f32[128,128]{1,0:T(8,128)S(1)} custom-call(f32[128,128]{1,0:T(8,128)S(1)} %cholesky.355), custom_call_target="Cholesky" | custom-call | tf_op jit(solution)/shard_map/jit(cholesky)/cholesky | solution.py:39
  489.0 9.8 %custom-call.23 = f32[1,128,128]{1,2,0:T(8,128)S(1)} custom-call(f32[1,128,128]{2,1,0:T(8,128)S(1)} %get-tuple-element.94), custom_call_target="InvertDiagBlocksLowerTriangular" | custom-call | tf_op jit(solution)/shard_map/jit(cholesky)/cholesky | solution.py:39
  499.3 11.7 %cholesky.333 = f32[128,128]{1,0:T(8,128)S(1)} custom-call(f32[128,128]{1,0:T(8,128)S(1)} %convolution_subtract_fusion.4), custom_call_target="Cholesky" | custom-call | tf_op jit(solution)/shard_map/jit(cholesky)/cholesky | solution.py:39
  513.8 4.1 while.11
  514.4 1.4 bitcast_dynamic-update-slice_fusion.11
  516.4 1.4 bitcast_dynamic-update-slice_fusion.11
  517.9 19.8 %custom-call.24 = f32[2,128,128]{1,2,0:T(8,128)S(1)} custom-call(f32[2,128,128]{2,1,0:T(8,128)S(1)} %get-tuple-element.34), custom_call_target="InvertDiagBlocksLowerTriangular" | custom-call | tf_op jit(solution)/shard_map/jit(_solve_triangular)/triangular_solve | solution.py:40
  538.7 11.7 %cholesky.282 = f32[128,128]{1,0:T(8,128)S(1)} custom-call(f32[128,128]{1,0:T(8,128)S(1)} %cholesky.352), custom_call_target="Cholesky" | custom-call | tf_op jit(solution)/shard_map/jit(cholesky)/cholesky | solution.py:39
  550.4 9.8 %custom-call.21 = f32[1,128,128]{1,2,0:T(8,128)S(1)} custom-call(f32[1,128,128]{2,1,0:T(8,128)S(1)} %get-tuple-element.98), custom_call_target="InvertDiagBlocksLowerTriangular" | custom-call | tf_op jit(solution)/shard_map/jit(cholesky)/cholesky | solution.py:39
  560.7 11.7 %cholesky.299 = f32[128,128]{1,0:T(8,128)S(1)} custom-call(f32[128,128]{1,0:T(8,128)S(1)} %convolution_subtract_fusion.5), custom_call_target="Cholesky" | custom-call | tf_op jit(solution)/shard_map/jit(cholesky)/cholesky | solution.py:39
  575.1 4.0 while.10
  575.7 1.4 bitcast_dynamic-update-slice_fusion.10
  577.7 1.4 bitcast_dynamic-update-slice_fusion.10
  579.1 19.9 %custom-call.22 = f32[2,128,128]{1,2,0:T(8,128)S(1)} custom-call(f32[2,128,128]{2,1,0:T(8,128)S(1)} %get-tuple-element.33), custom_call_target="InvertDiagBlocksLowerTriangular" | custom-call | tf_op jit(solution)/shard_map/jit(_solve_triangular)/triangular_solve | solution.py:40
  600.5 1.2 convolution_bitcast_fusion.4
  601.7 4.1 all-to-all-start.10
  605.8 1.1 fusion.33
  607.0 1.1 fusion.34
  608.1 8.9 %all-to-all-done.10 = f32[32,8,256]{2,1,0:T(8,128)S(1)} async-done(((f32[32,8,256]{2,1,0:T(8,128)}), f32[32,8,256]{2,1,0:T(8,128)S(1)}, u32[]{:S(2)}, u32[]{:S(2)}) %all-to-all-start.10) | async-done | bytes 262176 | tf_op jit(solution)/shard_map/all_to_all | solution.py:102
  (124 shorter events, 26.1 us)
Async XLA Ops:
  0.6 1.8 copy-start
  5.0 37.2 %all-to-all-start = ((f32[32,32,256]{2,1,0:T(8,128)}), f32[32,32,256]{2,1,0:T(8,128)S(1)}, u32[]{:S(2)}, u32[]{:S(2)}) async-start(f32[32,32,256]{2,1,0:T(8,128)} %pad_maximum_fusion.2), calls=%async_computation | async-start | bytes 2097152 | tf_op jit(solution)/shard_map/all_to_all | solution.py:28
  74.5 1.6 copy-start.1
  183.7 41.5 %all-to-all-start.5 = ((f32[32,48,256]{2,1,0:T(8,128)}), f32[32,48,256]{2,1,0:T(8,128)S(1)}, u32[]{:S(2)}, u32[]{:S(2)}) async-start(f32[32,48,256]{2,1,0:T(8,128)} %broadcast_in_dim.12), calls=%async_computation.5 | async-start | bytes 3145728 | tf_op jit(solution)/shard_map/all_to_all | solution.py:33
  227.9 0.7 copy-start.3
  291.3 1.2 copy-start.2
  456.2 20.6 %all-to-all-start.9 = ((f32[32,16,256]{2,1,0:T(8,128)}), f32[32,16,256]{2,1,0:T(8,128)S(1)}, u32[]{:S(2)}, u32[]{:S(2)}) async-start(f32[32,16,256]{2,1,0:T(8,128)} %broadcast_in_dim.15), calls=%async_computation.9 | async-start | bytes 1048576 | tf_op jit(solution)/shard_map/all_to_all | solution.py:33
  601.7 15.2 %all-to-all-start.10 = ((f32[32,8,256]{2,1,0:T(8,128)}), f32[32,8,256]{2,1,0:T(8,128)S(1)}, u32[]{:S(2)}, u32[]{:S(2)}) async-start(f32[32,8,256]{2,1,0:T(8,128)} %convolution_bitcast_fusion.4), calls=%async_computation.10 | async-start | bytes 524288 | tf_op jit(solution)/shard_map/all_to_all | solution.py:102

commit v2 on v1

v2 whole, which is shorter than its diff:
```python
import functools
import math

import jax
import jax.numpy as jnp
from jax import lax
from jax.experimental import pallas as pl
from jax.experimental.pallas import tpu as pltpu
from jax.sharding import PartitionSpec as P

PROJ_WIDTH = 8192
ITERS = 2
HIGH_PRECISION = lax.Precision.HIGHEST
F32 = jnp.float32
BF16 = jnp.bfloat16
LANES = 128
PANEL = 8


def mm(a, b, ca, cb):
    return lax.dot_general(
        a, b, (((ca,), (cb,)), ((), ())), precision=HIGH_PRECISION, preferred_element_type=F32
    )


def bmm(a, b, ca, cb):
    return lax.dot_general(
        a, b, (((ca,), (cb,)), ((0,), (0,))), precision=HIGH_PRECISION, preferred_element_type=F32
    )


def split3(a):
    a1 = a.astype(BF16).astype(F32)
    rest = a - a1
    a2 = rest.astype(BF16).astype(F32)
    return a1, a2, rest - a2


def inverse_factor_kernel(gram_ref, x_ref):
    n = gram_ref.shape[-1]
    x_ref[...] = gram_ref[...] * (1.0 / PROJ_WIDTH)
    lane = lax.broadcasted_iota(jnp.int32, (PANEL, n), 1)
    sub = lax.broadcasted_iota(jnp.int32, (PANEL, n), 0)
    widen = lambda v: jnp.concatenate([v] * (n // LANES), 1)
    for k in range(0, n, PANEL):
        end = k + PANEL
        panel = x_ref[k:end, :]
        rows = [jnp.broadcast_to(panel[r:r + 1, :], (PANEL, n)) for r in range(PANEL)]
        d = [
            [jnp.broadcast_to(rows[r][:, k + c:k + c + 1], (PANEL, LANES)) if c >= r else None
             for c in range(PANEL)]
            for r in range(PANEL)
        ]
        inside = (lane >= k) & (lane < end)
        rows = [
            jnp.where(inside, jnp.where(lane == k + r, 1.0, 0.0), rows[r]) for r in range(PANEL)
        ]
        for j in range(PANEL):
            s = lax.rsqrt(d[j][j])
            rows[j] = rows[j] * widen(s)
            u = [d[j][c] * s if c > j else None for c in range(PANEL)]
            for r in range(j + 1, PANEL):
                for c in range(r, PANEL):
                    d[r][c] = d[r][c] - u[r] * u[c]
                rows[r] = rows[r] - widen(u[r]) * rows[j]
        new = rows[PANEL - 1]
        for r in range(PANEL - 2, -1, -1):
            new = jnp.where(sub == r, rows[r], new)
        x_ref[k:end, :] = new
        if end < n:
            lo = end // LANES * LANES
            a = split3(jnp.where(lane >= end, new, 0.0)[:, lo:])
            b = split3(new)
            lhs = jnp.concatenate([a[0], a[0], a[1], a[1], a[0], a[2]], 0).astype(BF16)
            rhs = jnp.concatenate([b[0], b[1], b[0], b[1], b[2], b[0]], 0).astype(BF16)
            change = lax.dot_general(
                lhs, rhs, (((0,), (0,)), ((), ())), preferred_element_type=F32
            )
            old = x_ref[end:, :]
            at = lax.broadcasted_iota(jnp.int32, old.shape, 1)
            old = jnp.where((at >= k) & (at < end), 0.0, old)
            x_ref[end:, :] = old - change[end - lo:, :]
    row = lax.broadcasted_iota(jnp.int32, (n, n), 0)
    col = lax.broadcasted_iota(jnp.int32, (n, n), 1)
    x_ref[...] = jnp.where(col <= row, x_ref[...], 0.0)


def inverse_factor(gram):
    return pl.pallas_call(
        inverse_factor_kernel,
        out_shape=jax.ShapeDtypeStruct(gram.shape, F32),
        in_specs=[pl.BlockSpec(memory_space=pltpu.VMEM)],
        out_specs=pl.BlockSpec(memory_space=pltpu.VMEM),
    )(gram)


def exchange(chunks, axis, groups):
    return lax.all_to_all(chunks, axis, 0, 0, tiled=True, axis_index_groups=groups)


def scatter_sum(chunks, axis, groups):
    return jnp.sum(exchange(chunks, axis, groups), axis=0)


def gather(own, axis, groups):
    return exchange(jnp.broadcast_to(own[None], (len(groups[0]),) + own.shape), axis, groups)


def body(adapter_input_weight, adapter_output_weight, initial_output_basis, initial_input_basis):
    tenants, rank, feats = adapter_output_weight.shape
    r = initial_output_basis.shape[1]
    n_feat, n_tenant = lax.axis_size("feat"), lax.axis_size("tenant")
    chips = n_feat // 2
    core = lax.axis_index("feat") % 2
    same_core = [[2 * i + c for i in range(chips)] for c in range(2)]
    n_z = n_tenant // 2
    along_z = [[h * n_z + z for z in range(n_z)] for h in range(2)]
    swap_cores = [(i, i ^ 1) for i in range(n_feat)]
    swap_halves = [(i, (i + n_z) % n_tenant) for i in range(n_tenant)]
    root = 1.0 / math.sqrt(PROJ_WIDTH)
    mine = tenants // chips

    def pick(for_out, for_in):
        return jnp.where(core == 0, for_out, for_in)

    def to_partner(x):
        return lax.ppermute(x, "feat", swap_cores)

    w_out = adapter_output_weight.reshape(tenants * rank, feats)
    w_in = adapter_input_weight.reshape(tenants * rank, feats)
    sent = pick(
        jnp.concatenate([w_in, initial_input_basis], 0),
        jnp.concatenate([w_out, initial_output_basis], 0),
    )
    got = to_partner(sent)
    w = jnp.concatenate([pick(w_out, w_in), got[:tenants * rank]], 1)
    basis = jnp.concatenate([pick(initial_output_basis, initial_input_basis), got[tenants * rank:]], 0)

    partial = mm(w, basis, 1, 0).reshape(chips, mine * rank, r)
    p = (scatter_sum(partial, "feat", same_core) * root).reshape(mine, rank, r)
    other_gram = to_partner(bmm(p, p, 2, 2))
    factor = gather(bmm(other_gram, p, 2, 1).reshape(mine * rank, r), "feat", same_core)
    factor = factor.reshape(tenants * rank, r)

    for step in range(ITERS):
        part = mm(w, factor, 0, 0).reshape(n_z, 2 * feats // n_z, r)
        own = scatter_sum(part, "tenant", along_z)
        own = own + lax.ppermute(own, "tenant", swap_halves)
        raw = gather(own, "tenant", along_z).reshape(2 * feats, r)
        partial = mm(w, raw, 1, 0).reshape(chips, mine * rank, r)
        gram = mm(raw, raw, 0, 0).reshape(chips, r // chips, r)
        own = scatter_sum(jnp.concatenate([partial, gram], 1), "feat", same_core)
        if step < ITERS - 1:
            whole = gather(own, "feat", same_core)
            x = inverse_factor(whole[:, mine * rank:].reshape(r, r))
            p = mm(whole[:, :mine * rank].reshape(tenants * rank, r), x, 1, 1) * root
            p = p.reshape(tenants, rank, r)
            other_gram = to_partner(bmm(p, p, 2, 2))
            factor = bmm(other_gram, p, 2, 1).reshape(tenants * rank, r)
        else:
            x = inverse_factor(gather(own[mine * rank:], "feat", same_core).reshape(r, r))
            p = (mm(own[:mine * rank], x, 1, 1) * root).reshape(mine, rank, r)
            other = to_partner(p)
            p_out, p_in = pick(p, other), pick(other, p)
            rows = p_out.reshape(mine, rank, chips, 2, r // n_feat)
            rows = pick(rows[:, :, :, 0], rows[:, :, :, 1]).reshape(mine, rank, r // 2)
            made = bmm(rows, p_in, 1, 1).reshape(mine, chips, r // n_feat, r)
            cores = exchange(made.transpose(1, 0, 2, 3), "feat", same_core)
            cores = cores.reshape(tenants, r // n_feat, r)
            away = to_partner(mm(raw[feats:], x, 1, 1))
            here = mm(raw[:feats], x, 1, 1)
    return cores, pick(here, away), pick(away, here)


def solution(mesh):
    placed = (
        P("tenant", None, "feat"),
        P("tenant", None, "feat"),
        P("feat", None),
        P("feat", None),
    )
    return jax.shard_map(
        body,
        mesh=mesh,
        in_specs=placed,
        out_specs=(P("tenant", "feat", None), P("feat", None), P("feat", None)),
        check_vma=False,
    )
```

time: 627 us -> 307 us (0.49); the launches traced: 618 us -> 306 us
  other arithmetic: 220 us -> 2.32 us
  blocking collectives: 225 us -> 165 us
  waiting for transfers between devices: 88.7 us -> 43.3 us
  Pallas kernels: 0 us -> 27.4 us
  starting transfers between devices: 23.5 us -> 48.2 us
  matrix products: 30 us -> 12.6 us
  local copies, waits for them, and re-layouts: 23.7 us -> 6.49 us
    another operation x35 -> x0, other arithmetic: 217 us -> none  [the longest x26 137 us: inverse_factor(): lower_factor = jnp.linalg.cholesky(gram_matrix / PROJ_WIDTH)]
    all_to_all x7 -> x8, blocking collectives: 225 us -> 165 us  [exchange(): lax.all_to_all(chunks, axis, 0, 0, tiled=True, axis_index_groups=groups)]
    all_to_all x4 -> x3, waiting for transfers between devices: 88.7 us -> 31.3 us  [exchange(): lax.all_to_all(chunks, axis, 0, 0, tiled=True, axis_index_groups=groups)]
    ppermute x0 -> x7, starting transfers between devices: none -> 34.5 us  [the longest x5 24.9 us: to_partner(): return lax.ppermute(x, 'feat', swap_cores)]
    pallas_call x0 -> x2, Pallas kernels: none -> 27.4 us  [inverse_factor(): pl.pallas_call(inverse_factor_kernel, out_shape=jax.ShapeDtypeStruct(gram...]
    another operation x37 -> x0, local copies, waits for them, and re-layouts: 16.2 us -> none  [the longest x29 16.1 us: inverse_factor(): jax.scipy.linalg.solve_triangular(lower_factor, jnp.eye(gram_matrix.shape...]
    ppermute x0 -> x7, waiting for transfers between devices: none -> 12 us  [the longest x2 8.31 us: body(): own = own + lax.ppermute(own, 'tenant', swap_halves)]
    dot_general x25 -> x11, matrix products: 20.6 us -> 10.7 us  [mm(): lax.dot_general(a, b, (((ca,), (cb,)), ((), ())), precision=HIGH_PRECISIO...]
  transfers between devices with their start and end apart: 4 -> 10, of which waited for: 4 -> 8; matrix products, arithmetic and copies ran while one was open for 0% -> 1% of each run, Pallas kernels for 0% -> 0%
where the time goes in v2:
time: 307 us; the launch traced here: 306 us
  blocking collectives  165 us (54%)
  starting transfers between devices  48.2 us (16%)
  waiting for transfers between devices  43.3 us (14%)
  Pallas kernels  27.4 us (9%)
  matrix products  12.6 us (4%)
  local copies, waits for them, and re-layouts  6.49 us (2%)
    all_to_all x8, blocking collectives, exchange(): lax.all_to_all(chunks, axis, 0, 0, tiled=True, axis_index_groups=groups)  165 us
    all_to_all x3, waiting for transfers between devices, exchange(): lax.all_to_all(chunks, axis, 0, 0, tiled=True, axis_index_groups=groups)  31.3 us
    pallas_call x2, Pallas kernels, inverse_factor(): pl.pallas_call(inverse_factor_kernel, out_shape=jax.ShapeDtypeStruct(gram...  27.4 us
    ppermute x5, starting transfers between devices, to_partner(): return lax.ppermute(x, 'feat', swap_cores)  24.9 us
    all_to_all x3, starting transfers between devices, exchange(): lax.all_to_all(chunks, axis, 0, 0, tiled=True, axis_index_groups=groups)  13.8 us
    dot_general x11, matrix products, mm(): lax.dot_general(a, b, (((ca,), (cb,)), ((), ())), precision=HIGH_PRECISIO...  10.7 us
    ppermute x2, starting transfers between devices, body(): own = own + lax.ppermute(own, 'tenant', swap_halves)  9.51 us
    ppermute x2, waiting for transfers between devices, body(): own = own + lax.ppermute(own, 'tenant', swap_halves)  8.31 us
  transfers between devices with their start and end apart: 10, of which 8 were waited for; matrix products, arithmetic and copies ran while one was open for 1% of the time, Pallas kernels for 0%

profile of v2, /device:TPU:1, one launch (start us, length us, event | category | flops | bytes accessed | tf_op | source)
XLA Modules:
  0.0 306.1 jit_solution(5674172100112508483)
XLA Ops:
  0.7 1.5 maximum_select_fusion
  2.2 0.0 copy-start.1
  2.2 8.9 %collective-permute-start = (f32[768,256]{1,0:T(8,128)S(1)}, f32[768,256]{1,0:T(8,128)S(1)}, u32[]{:S(2)}, u32[]{:S(2)}) collective-permute-start(f32[768,256]{1,0:T(8,128)S(1)} %maximum_select_fusion), channel_id=1, source_target_pairs={{0,1},{1,0},{2,3},{3,2},{4,5},{5,4},{6,7},{7,6},{8,9},{9,8},{10,11... | collective-permute-start | bytes 2359304 | tf_op jit(solution)/shard_map/ppermute | solution.py:127
  11.2 0.1 broadcast_select_fusion
  11.3 1.7 collective-permute-done
  13.1 1.0 fusion
  14.1 17.0 %all_to_all.55 = f32[16,32,256]{2,1,0:T(8,128)S(1)} all-to-all(f32[16,32,256]{2,1,0:T(8,128)S(1)} %bitcast.91), channel_id=1, replica_groups={{0,2,4,6,8,10,12,14,16,18,20,22,24,26,28,30},{1,3,5,7,9,11,13,15,17,19,..., dimensions={0} | all-to-all | bytes 1048576 | tf_op jit(solution)/shard_map/all_to_all | solution.py:98
  31.2 0.2 fusion.14
  31.3 3.7 %collective-permute-start.1 = (f32[2,16,16]{2,1,0:T(8,128)S(1)}, f32[2,16,16]{2,1,0:T(8,128)S(1)}, u32[]{:S(2)}, u32[]{:S(2)}) collective-permute-start(f32[2,16,16]{2,1,0:T(8,128)S(1)} %fusion.14), channel_id=1, source_target_pairs={{0,1},{1,0},{2,3},{3,2},{4,5},{5,4},{6,7},{7,6},{8,9},{9,8},{10,11... | collective-permute-start | bytes 6152 | tf_op jit(solution)/shard_map/ppermute | solution.py:127
  35.1 0.8 collective-permute-done.1
  35.9 0.2 fusion.15
  36.0 0.9 broadcast_in_dim.13
  36.9 4.4 %all-to-all-start.1 = ((f32[16,32,256]{2,1,0:T(8,128)}), f32[16,32,256]{2,1,0:T(8,128)}, u32[]{:S(2)}, u32[]{:S(2)}) async-start(f32[16,32,256]{2,1,0:T(8,128)} %broadcast_in_dim.13), calls=%async_computation.1 | async-start | bytes 1048576 | tf_op jit(solution)/shard_map/all_to_all | solution.py:98
  41.3 0.3 pad_maximum_fusion
  41.5 0.3 copy.22
  41.9 13.6 %all-to-all-done.1 = f32[16,32,256]{2,1,0:T(8,128)} async-done(((f32[16,32,256]{2,1,0:T(8,128)}), f32[16,32,256]{2,1,0:T(8,128)}, u32[]{:S(2)}, u32[]{:S(2)}) %all-to-all-start.1) | async-done | bytes 524320 | tf_op jit(solution)/shard_map/all_to_all | solution.py:98
  55.5 2.0 fusion.16
  57.5 23.3 %all_to_all.56 = f32[8,64,256]{2,1,0:T(8,128)S(1)} all-to-all(f32[8,64,256]{2,1,0:T(8,128)S(1)} %fusion.16), channel_id=1, replica_groups={{0,32,64,96,128,160,192,224},{256,288,320,352,384,416,448,480},{1,33,65..., dimensions={0} | all-to-all | bytes 1048576 | tf_op jit(solution)/shard_map/all_to_all | solution.py:98
  80.8 4.8 %collective-permute-start.2 = (f32[64,256]{1,0:T(8,128)S(1)}, f32[64,256]{1,0:T(8,128)S(1)}, u32[]{:S(2)}, u32[]{:S(2)}) collective-permute-start(f32[64,256]{1,0:T(8,128)S(1)} %reduce_sum.46), channel_id=1, source_target_pairs={{0,256},{32,288},{64,320},{96,352},{128,384},{160,416},{192,448},{... | collective-permute-start | bytes 196616 | tf_op jit(solution)/shard_map/ppermute | solution.py:148
  85.6 4.2 %collective-permute-done.2 = f32[64,256]{1,0:T(8,128)S(1)} collective-permute-done((f32[64,256]{1,0:T(8,128)S(1)}, f32[64,256]{1,0:T(8,128)S(1)}, u32[]{:S(2)}, u32[]{:S(2)}) %collective-permute-start.2) | collective-permute-done | bytes 65568 | tf_op jit(solution)/shard_map/ppermute | solution.py:148
  89.8 15.6 %all_to_all.57 = f32[8,64,256]{2,1,0:T(8,128)S(1)} all-to-all(f32[8,64,256]{2,1,0:T(8,128)S(1)} %broadcast_in_dim.14), channel_id=1, replica_groups={{0,32,64,96,128,160,192,224},{256,288,320,352,384,416,448,480},{1,33,65..., dimensions={0} | all-to-all | bytes 1048576 | tf_op jit(solution)/shard_map/all_to_all | solution.py:98
  105.4 0.2 copy.23
  105.6 0.6 fusion.18
  106.2 1.0 fusion.17
  107.2 0.1 pad_maximum_fusion.1
  107.3 22.9 %all_to_all.58 = f32[16,48,256]{2,1,0:T(8,128)S(1)} all-to-all(f32[16,48,256]{2,1,0:T(8,128)S(1)} %pad_maximum_fusion.1), channel_id=1, replica_groups={{0,2,4,6,8,10,12,14,16,18,20,22,24,26,28,30},{1,3,5,7,9,11,13,15,17,19,..., dimensions={0} | all-to-all | bytes 1572864 | tf_op jit(solution)/shard_map/all_to_all | solution.py:98
  130.1 0.1 reduce_sum.47
  130.2 0.1 broadcast_in_dim.15
  130.3 26.0 %all_to_all.59 = f32[16,48,256]{2,1,0:T(8,128)S(1)} all-to-all(f32[16,48,256]{2,1,0:T(8,128)S(1)} %broadcast_in_dim.15), channel_id=1, replica_groups={{0,2,4,6,8,10,12,14,16,18,20,22,24,26,28,30},{1,3,5,7,9,11,13,15,17,19,..., dimensions={0} | all-to-all | bytes 1572864 | tf_op jit(solution)/shard_map/all_to_all | solution.py:98
  156.2 0.7 slice.51
  157.0 13.7 %shard_map.67 = f32[256,256]{1,0:T(8,128)} custom-call(f32[256,256]{1,0:T(8,128)} %bitcast.96), custom_call_target="tpu_custom_call" | custom-call | tf_op jit(solution)/shard_map/pallas_call | solution.py:89
  170.7 0.9 copy-done.3
  171.6 0.6 convolution_multiply_fusion
  172.2 0.6 fusion.19
  172.8 4.8 %collective-permute-start.3 = (f32[32,16,16]{2,1,0:T(8,128)S(1)}, f32[32,16,16]{2,1,0:T(8,128)S(1)}, u32[]{:S(2)}, u32[]{:S(2)}) collective-permute-start(f32[32,16,16]{2,1,0:T(8,128)S(1)} %fusion.19), channel_id=1, source_target_pairs={{0,1},{1,0},{2,3},{3,2},{4,5},{5,4},{6,7},{7,6},{8,9},{9,8},{10,11... | collective-permute-start | bytes 98312 | tf_op jit(solution)/shard_map/ppermute | solution.py:127
  177.6 1.1 collective-permute-done.3
  178.7 0.6 fusion.20
  179.3 1.0 fusion.21
  180.3 21.6 %all_to_all.60 = f32[8,64,256]{2,1,0:T(8,128)S(1)} all-to-all(f32[8,64,256]{2,1,0:T(8,128)S(1)} %fusion.21), channel_id=1, replica_groups={{0,32,64,96,128,160,192,224},{256,288,320,352,384,416,448,480},{1,33,65..., dimensions={0} | all-to-all | bytes 1048576 | tf_op jit(solution)/shard_map/all_to_all | solution.py:98
  201.9 4.8 %collective-permute-start.4 = (f32[64,256]{1,0:T(8,128)S(1)}, f32[64,256]{1,0:T(8,128)S(1)}, u32[]{:S(2)}, u32[]{:S(2)}) collective-permute-start(f32[64,256]{1,0:T(8,128)S(1)} %reduce_sum.48), channel_id=1, source_target_pairs={{0,256},{32,288},{64,320},{96,352},{128,384},{160,416},{192,448},{... | collective-permute-start | bytes 196616 | tf_op jit(solution)/shard_map/ppermute | solution.py:148
  206.7 4.2 %collective-permute-done.4 = f32[64,256]{1,0:T(8,128)S(1)} collective-permute-done((f32[64,256]{1,0:T(8,128)S(1)}, f32[64,256]{1,0:T(8,128)S(1)}, u32[]{:S(2)}, u32[]{:S(2)}) %collective-permute-start.4) | collective-permute-done | bytes 65568 | tf_op jit(solution)/shard_map/ppermute | solution.py:148
  210.9 16.2 %all_to_all.61 = f32[8,64,256]{2,1,0:T(8,128)S(1)} all-to-all(f32[8,64,256]{2,1,0:T(8,128)S(1)} %broadcast_in_dim.16), channel_id=1, replica_groups={{0,32,64,96,128,160,192,224},{256,288,320,352,384,416,448,480},{1,33,65..., dimensions={0} | all-to-all | bytes 1048576 | tf_op jit(solution)/shard_map/all_to_all | solution.py:98
  227.0 1.0 fusion.22
  228.0 0.2 copy.24
  228.2 0.6 fusion.23
  228.8 0.1 pad_maximum_fusion.2
  228.9 22.2 %all_to_all.62 = f32[16,48,256]{2,1,0:T(8,128)S(1)} all-to-all(f32[16,48,256]{2,1,0:T(8,128)S(1)} %pad_maximum_fusion.2), channel_id=1, replica_groups={{0,2,4,6,8,10,12,14,16,18,20,22,24,26,28,30},{1,3,5,7,9,11,13,15,17,19,..., dimensions={0} | all-to-all | bytes 1572864 | tf_op jit(solution)/shard_map/all_to_all | solution.py:98
  251.1 0.1 reduce_sum.49
  251.2 0.7 broadcast_in_dim.17
  251.9 5.9 %all-to-all-start.9 = ((f32[16,16,256]{2,1,0:T(8,128)}), f32[16,16,256]{2,1,0:T(8,128)S(1)}, u32[]{:S(2)}, u32[]{:S(2)}) async-start(f32[16,16,256]{2,1,0:T(8,128)} %broadcast_in_dim.17), calls=%async_computation.9 | async-start | bytes 524288 | tf_op jit(solution)/shard_map/all_to_all | solution.py:98
  257.9 8.8 %all-to-all-done.9 = f32[16,16,256]{2,1,0:T(8,128)S(1)} async-done(((f32[16,16,256]{2,1,0:T(8,128)}), f32[16,16,256]{2,1,0:T(8,128)S(1)}, u32[]{:S(2)}, u32[]{:S(2)}) %all-to-all-start.9) | async-done | bytes 262176 | tf_op jit(solution)/shard_map/all_to_all | solution.py:98
  266.7 0.7 copy-done.6
  267.4 13.7 %shard_map.68 = f32[256,256]{1,0:T(8,128)} custom-call(f32[256,256]{1,0:T(8,128)} %bitcast.95), custom_call_target="tpu_custom_call" | custom-call | tf_op jit(solution)/shard_map/pallas_call | solution.py:89
  281.1 1.4 convolution_multiply_fusion.1
  282.5 0.1 copy.26
  282.6 5.6 %collective-permute-start.5 = (f32[2,16,256]{1,2,0:T(8,128)S(1)}, f32[2,16,256]{1,2,0:T(8,128)S(1)}, u32[]{:S(2)}, u32[]{:S(2)}) collective-permute-start(f32[2,16,256]{1,2,0:T(8,128)S(1)} %copy.26), channel_id=1, source_target_pairs={{0,1},{1,0},{2,3},{3,2},{4,5},{5,4},{6,7},{7,6},{8,9},{9,8},{10,11... | collective-permute-start | bytes 98312 | tf_op jit(solution)/shard_map/ppermute | solution.py:127
  288.3 0.4 fusion.24
  288.7 1.9 collective-permute-start.6
  290.7 0.4 convolution_bitcast_fusion
  291.1 0.7 copy.34
  291.8 3.5 %all-to-all-start.10 = ((f32[16,2,8,256]{3,2,1,0:T(8,128)}), f32[16,2,8,256]{3,2,1,0:T(8,128)S(1)}, u32[]{:S(2)}, u32[]{:S(2)}) async-start(f32[16,2,8,256]{3,2,1,0:T(8,128)} %bitcast.72), calls=%async_computation.10 | async-start | bytes 524288 | tf_op jit(solution)/shard_map/all_to_all | solution.py:98
  295.3 1.2 broadcast_select_fusion.1
  296.6 8.8 %all-to-all-done.10 = f32[16,2,8,256]{3,2,1,0:T(8,128)S(1)} async-done(((f32[16,2,8,256]{3,2,1,0:T(8,128)}), f32[16,2,8,256]{3,2,1,0:T(8,128)S(1)}, u32[]{:S(2)}, u32[]{:S(2)}) %all-to-all-start.10) | async-done | bytes 262176 | tf_op jit(solution)/shard_map/all_to_all | solution.py:98
  305.4 0.7 copy.36
  (28 shorter events, 0.4 us)
Async XLA Ops:
  0.6 10.5 %copy-start.4 = (f32[256,256]{1,0:T(8,128)S(1)}, f32[256,256]{1,0:T(8,128)}, u32[]{:S(2)}) copy-start(f32[256,256]{1,0:T(8,128)} %param.7) | copy-start | bytes 786436
  0.7 10.5 %copy-start.5 = (f32[256,256]{1,0:T(8,128)S(1)}, f32[256,256]{1,0:T(8,128)}, u32[]{:S(2)}) copy-start(f32[256,256]{1,0:T(8,128)} %param.6) | copy-start | bytes 786436
  0.7 10.6 %copy-start.2 = (f32[32,16,256]{2,1,0:T(8,128)S(1)}, f32[32,16,256]{2,1,0:T(8,128)}, u32[]{:S(2)}) copy-start(f32[32,16,256]{2,1,0:T(8,128)} %param.5) | copy-start | bytes 1572868
  2.2 9.0 %copy-start.1 = (f32[32,16,256]{2,1,0:T(8,128)S(1)}, f32[32,16,256]{2,1,0:T(8,128)}, u32[]{:S(2)}) copy-start(f32[32,16,256]{2,1,0:T(8,128)} %param.4) | copy-start | bytes 1572868
  2.2 10.8 %collective-permute-start = (f32[768,256]{1,0:T(8,128)S(1)}, f32[768,256]{1,0:T(8,128)S(1)}, u32[]{:S(2)}, u32[]{:S(2)}) collective-permute-start(f32[768,256]{1,0:T(8,128)S(1)} %maximum_select_fusion), channel_id=1, source_target_pairs={{0,1},{1,0},{2,3},{3,2},{4,5},{5,4},{6,7},{7,6},{8,9},{9,8},{10,11... | collective-permute-start | bytes 2359304 | tf_op jit(solution)/shard_map/ppermute | solution.py:127
  31.3 4.6 %collective-permute-start.1 = (f32[2,16,16]{2,1,0:T(8,128)S(1)}, f32[2,16,16]{2,1,0:T(8,128)S(1)}, u32[]{:S(2)}, u32[]{:S(2)}) collective-permute-start(f32[2,16,16]{2,1,0:T(8,128)S(1)} %fusion.14), channel_id=1, source_target_pairs={{0,1},{1,0},{2,3},{3,2},{4,5},{5,4},{6,7},{7,6},{8,9},{9,8},{10,11... | collective-permute-start | bytes 6152 | tf_op jit(solution)/shard_map/ppermute | solution.py:127
  36.9 18.6 %all-to-all-start.1 = ((f32[16,32,256]{2,1,0:T(8,128)}), f32[16,32,256]{2,1,0:T(8,128)}, u32[]{:S(2)}, u32[]{:S(2)}) async-start(f32[16,32,256]{2,1,0:T(8,128)} %broadcast_in_dim.13), calls=%async_computation.1 | async-start | bytes 1048576 | tf_op jit(solution)/shard_map/all_to_all | solution.py:98
  80.8 8.9 %collective-permute-start.2 = (f32[64,256]{1,0:T(8,128)S(1)}, f32[64,256]{1,0:T(8,128)S(1)}, u32[]{:S(2)}, u32[]{:S(2)}) collective-permute-start(f32[64,256]{1,0:T(8,128)S(1)} %reduce_sum.46), channel_id=1, source_target_pairs={{0,256},{32,288},{64,320},{96,352},{128,384},{160,416},{192,448},{... | collective-permute-start | bytes 196616 | tf_op jit(solution)/shard_map/ppermute | solution.py:148
  170.7 0.9 copy-start.3
  172.8 5.9 %collective-permute-start.3 = (f32[32,16,16]{2,1,0:T(8,128)S(1)}, f32[32,16,16]{2,1,0:T(8,128)S(1)}, u32[]{:S(2)}, u32[]{:S(2)}) collective-permute-start(f32[32,16,16]{2,1,0:T(8,128)S(1)} %fusion.19), channel_id=1, source_target_pairs={{0,1},{1,0},{2,3},{3,2},{4,5},{5,4},{6,7},{7,6},{8,9},{9,8},{10,11... | collective-permute-start | bytes 98312 | tf_op jit(solution)/shard_map/ppermute | solution.py:127
  201.9 8.9 %collective-permute-start.4 = (f32[64,256]{1,0:T(8,128)S(1)}, f32[64,256]{1,0:T(8,128)S(1)}, u32[]{:S(2)}, u32[]{:S(2)}) collective-permute-start(f32[64,256]{1,0:T(8,128)S(1)} %reduce_sum.48), channel_id=1, source_target_pairs={{0,256},{32,288},{64,320},{96,352},{128,384},{160,416},{192,448},{... | collective-permute-start | bytes 196616 | tf_op jit(solution)/shard_map/ppermute | solution.py:148
  251.9 14.8 %all-to-all-start.9 = ((f32[16,16,256]{2,1,0:T(8,128)}), f32[16,16,256]{2,1,0:T(8,128)S(1)}, u32[]{:S(2)}, u32[]{:S(2)}) async-start(f32[16,16,256]{2,1,0:T(8,128)} %broadcast_in_dim.17), calls=%async_computation.9 | async-start | bytes 524288 | tf_op jit(solution)/shard_map/all_to_all | solution.py:98
  266.7 0.7 copy-start.6
  281.1 7.1 %copy-start = (f32[256,256]{1,0:T(8,128)S(1)}, f32[256,256]{1,0:T(8,128)}, u32[]{:S(2)}) copy-start(f32[256,256]{1,0:T(8,128)} %shard_map.68) | copy-start | bytes 786436
  282.6 8.0 %collective-permute-start.5 = (f32[2,16,256]{1,2,0:T(8,128)S(1)}, f32[2,16,256]{1,2,0:T(8,128)S(1)}, u32[]{:S(2)}, u32[]{:S(2)}) collective-permute-start(f32[2,16,256]{1,2,0:T(8,128)S(1)} %copy.26), channel_id=1, source_target_pairs={{0,1},{1,0},{2,3},{3,2},{4,5},{5,4},{6,7},{7,6},{8,9},{9,8},{10,11... | collective-permute-start | bytes 98312 | tf_op jit(solution)/shard_map/ppermute | solution.py:127
  288.7 6.7 %collective-permute-start.6 = (f32[256,256]{1,0:T(8,128)S(1)}, f32[256,256]{1,0:T(8,128)S(1)}, u32[]{:S(2)}, u32[]{:S(2)}) collective-permute-start(f32[256,256]{1,0:T(8,128)S(1)} %fusion.24), channel_id=1, source_target_pairs={{0,1},{1,0},{2,3},{3,2},{4,5},{5,4},{6,7},{7,6},{8,9},{9,8},{10,11... | collective-permute-start | bytes 786440 | tf_op jit(solution)/shard_map/ppermute | solution.py:127
  291.8 13.6 %all-to-all-start.10 = ((f32[16,2,8,256]{3,2,1,0:T(8,128)}), f32[16,2,8,256]{3,2,1,0:T(8,128)S(1)}, u32[]{:S(2)}, u32[]{:S(2)}) async-start(f32[16,2,8,256]{3,2,1,0:T(8,128)} %bitcast.72), calls=%async_computation.10 | async-start | bytes 524288 | tf_op jit(solution)/shard_map/all_to_all | solution.py:98

commit v3 on v2

--- a/solution.py
+++ b/solution.py
@@ -42,13 +42,18 @@
     lane = lax.broadcasted_iota(jnp.int32, (PANEL, n), 1)
     sub = lax.broadcasted_iota(jnp.int32, (PANEL, n), 0)
     widen = lambda v: jnp.concatenate([v] * (n // LANES), 1)
+    spread = lambda row, at: jnp.broadcast_to(row[:, at:at + 1], (PANEL, LANES))
+    before = None
     for k in range(0, n, PANEL):
         end = k + PANEL
         panel = x_ref[k:end, :]
         rows = [jnp.broadcast_to(panel[r:r + 1, :], (PANEL, n)) for r in range(PANEL)]
+        if before is not None:
+            rows = [jnp.where((lane >= k - PANEL) & (lane < k), 0.0, row) for row in rows]
+            for y in before:
+                rows = [row - widen(spread(y, k + r)) * y for r, row in enumerate(rows)]
         d = [
-            [jnp.broadcast_to(rows[r][:, k + c:k + c + 1], (PANEL, LANES)) if c >= r else None
-             for c in range(PANEL)]
+            [spread(rows[r], k + c) if c >= r else None for c in range(PANEL)]
             for r in range(PANEL)
         ]
         inside = (lane >= k) & (lane < end)
@@ -67,19 +72,21 @@
         for r in range(PANEL - 2, -1, -1):
             new = jnp.where(sub == r, rows[r], new)
         x_ref[k:end, :] = new
-        if end < n:
-            lo = end // LANES * LANES
-            a = split3(jnp.where(lane >= end, new, 0.0)[:, lo:])
+        before = rows
+        rest = end + PANEL
+        if rest < n:
+            lo = rest // LANES * LANES
+            a = split3(jnp.where(lane >= rest, new, 0.0)[:, lo:])
             b = split3(new)
             lhs = jnp.concatenate([a[0], a[0], a[1], a[1], a[0], a[2]], 0).astype(BF16)
             rhs = jnp.concatenate([b[0], b[1], b[0], b[1], b[2], b[0]], 0).astype(BF16)
             change = lax.dot_general(
                 lhs, rhs, (((0,), (0,)), ((), ())), preferred_element_type=F32
             )
-            old = x_ref[end:, :]
+            old = x_ref[rest:, :]
             at = lax.broadcasted_iota(jnp.int32, old.shape, 1)
             old = jnp.where((at >= k) & (at < end), 0.0, old)
-            x_ref[end:, :] = old - change[end - lo:, :]
+            x_ref[rest:, :] = old - change[rest - lo:, :]
     row = lax.broadcasted_iota(jnp.int32, (n, n), 0)
     col = lax.broadcasted_iota(jnp.int32, (n, n), 1)
     x_ref[...] = jnp.where(col <= row, x_ref[...], 0.0)
@@ -143,32 +150,35 @@
     factor = factor.reshape(tenants * rank, r)
 
     for step in range(ITERS):
-        part = mm(w, factor, 0, 0).reshape(n_z, 2 * feats // n_z, r)
-        own = scatter_sum(part, "tenant", along_z)
+        part = mm(w, factor, 0, 0)
+        own = scatter_sum(part.reshape(n_z, 2 * feats // n_z, r), "tenant", along_z)
         own = own + lax.ppermute(own, "tenant", swap_halves)
         raw = gather(own, "tenant", along_z).reshape(2 * feats, r)
         partial = mm(w, raw, 1, 0).reshape(chips, mine * rank, r)
         gram = mm(raw, raw, 0, 0).reshape(chips, r // chips, r)
         own = scatter_sum(jnp.concatenate([partial, gram], 1), "feat", same_core)
+        whole = gather(own, "feat", same_core)
+        x = inverse_factor(whole[:, mine * rank:].reshape(r, r))
+        p = mm(whole[:, :mine * rank].reshape(tenants * rank, r), x, 1, 1) * root
         if step < ITERS - 1:
-            whole = gather(own, "feat", same_core)
-            x = inverse_factor(whole[:, mine * rank:].reshape(r, r))
-            p = mm(whole[:, :mine * rank].reshape(tenants * rank, r), x, 1, 1) * root
             p = p.reshape(tenants, rank, r)
             other_gram = to_partner(bmm(p, p, 2, 2))
             factor = bmm(other_gram, p, 2, 1).reshape(tenants * rank, r)
-        else:
-            x = inverse_factor(gather(own[mine * rank:], "feat", same_core).reshape(r, r))
-            p = (mm(own[:mine * rank], x, 1, 1) * root).reshape(mine, rank, r)
-            other = to_partner(p)
-            p_out, p_in = pick(p, other), pick(other, p)
-            rows = p_out.reshape(mine, rank, chips, 2, r // n_feat)
-            rows = pick(rows[:, :, :, 0], rows[:, :, :, 1]).reshape(mine, rank, r // 2)
-            made = bmm(rows, p_in, 1, 1).reshape(mine, chips, r // n_feat, r)
-            cores = exchange(made.transpose(1, 0, 2, 3), "feat", same_core)
-            cores = cores.reshape(tenants, r // n_feat, r)
-            away = to_partner(mm(raw[feats:], x, 1, 1))
-            here = mm(raw[:feats], x, 1, 1)
+    other = to_partner(p)
+    away = to_partner(mm(raw[feats:], x, 1, 1))
+    here = mm(raw[:feats], x, 1, 1)
+    n_rows = r // n_feat
+    first = lax.axis_index("feat") * n_rows
+    one_hot = lax.broadcasted_iota(jnp.int32, (n_rows, r), 1) == (
+        first + lax.broadcasted_iota(jnp.int32, (n_rows, r), 0)
+    )
+    cols = mm(one_hot.astype(F32), pick(p, other), 1, 1)
+    shape = (tenants, n_rows, tenants * rank)
+    own_tenant = lax.broadcasted_iota(jnp.int32, shape, 2) // rank == lax.broadcasted_iota(
+        jnp.int32, shape, 0
+    )
+    blocks = jnp.where(own_tenant, cols[None], 0.0).reshape(tenants * n_rows, tenants * rank)
+    cores = mm(blocks, pick(other, p), 1, 0).reshape(tenants, n_rows, r)
     return cores, pick(here, away), pick(away, here)
 
 

time: 307 us -> 296 us (0.964)
  Pallas kernels: 27.4 us -> 19.8 us
    pallas_call x2, Pallas kernels: 27.4 us -> 19.8 us  [inverse_factor(): pl.pallas_call(inverse_factor_kernel, out_shape=jax.ShapeDtypeStruct(gram...]
    all_to_all x3 -> x2, starting transfers between devices: 13.8 us -> 9.68 us  [exchange(): lax.all_to_all(chunks, axis, 0, 0, tiled=True, axis_index_groups=groups)]
    all_to_all x3 -> x2, waiting for transfers between devices: 31.3 us -> 29.6 us  [exchange(): lax.all_to_all(chunks, axis, 0, 0, tiled=True, axis_index_groups=groups)]
    dot_general x11 -> x13, matrix products: 10.7 us -> 11.7 us  [mm(): lax.dot_general(a, b, (((ca,), (cb,)), ((), ())), precision=HIGH_PRECISIO...]
  transfers between devices with their start and end apart: 10 -> 9, of which waited for: 8 -> 8; matrix products, arithmetic and copies ran while one was open for 1% -> 1% of each run, Pallas kernels for 0% -> 0%
where the time goes in v3:
time: 296 us; the launch traced here: 295 us
  blocking collectives  164 us (55%)
  starting transfers between devices  45.9 us (16%)
  waiting for transfers between devices  42.2 us (14%)
  Pallas kernels  19.8 us (7%)
  matrix products  13.2 us (4%)
  local copies, waits for them, and re-layouts  6.13 us (2%)
    all_to_all x8, blocking collectives, exchange(): lax.all_to_all(chunks, axis, 0, 0, tiled=True, axis_index_groups=groups)  164 us
    all_to_all x2, waiting for transfers between devices, exchange(): lax.all_to_all(chunks, axis, 0, 0, tiled=True, axis_index_groups=groups)  29.6 us
    ppermute x5, starting transfers between devices, to_partner(): return lax.ppermute(x, 'feat', swap_cores)  26.7 us
    pallas_call x2, Pallas kernels, inverse_factor(): pl.pallas_call(inverse_factor_kernel, out_shape=jax.ShapeDtypeStruct(gram...  19.8 us
    dot_general x13, matrix products, mm(): lax.dot_general(a, b, (((ca,), (cb,)), ((), ())), precision=HIGH_PRECISIO...  11.7 us
    all_to_all x2, starting transfers between devices, exchange(): lax.all_to_all(chunks, axis, 0, 0, tiled=True, axis_index_groups=groups)  9.68 us
    ppermute x2, starting transfers between devices, body(): own = own + lax.ppermute(own, 'tenant', swap_halves)  9.51 us
    ppermute x2, waiting for transfers between devices, body(): own = own + lax.ppermute(own, 'tenant', swap_halves)  8.31 us
  transfers between devices with their start and end apart: 9, of which 8 were waited for; matrix products, arithmetic and copies ran while one was open for 1% of the time, Pallas kernels for 0%

profile of v3, /device:TPU:1, one launch (start us, length us, event | category | flops | bytes accessed | tf_op | source)
XLA Modules:
  0.0 294.6 jit_solution(5620699212702958867)
XLA Ops:
  0.6 0.0 copy-start.4
  0.7 1.5 maximum_select_fusion
  2.2 0.0 copy-start.1
  2.2 8.9 %collective-permute-start = (f32[768,256]{1,0:T(8,128)S(1)}, f32[768,256]{1,0:T(8,128)S(1)}, u32[]{:S(2)}, u32[]{:S(2)}) collective-permute-start(f32[768,256]{1,0:T(8,128)S(1)} %maximum_select_fusion), channel_id=1, source_target_pairs={{0,1},{1,0},{2,3},{3,2},{4,5},{5,4},{6,7},{7,6},{8,9},{9,8},{10,11... | collective-permute-start | bytes 2359304 | tf_op jit(solution)/shard_map/ppermute | solution.py:134
  11.2 0.1 broadcast_select_fusion
  11.3 1.7 collective-permute-done
  13.1 1.0 fusion
  14.1 17.0 %all_to_all.50 = f32[16,32,256]{2,1,0:T(8,128)S(1)} all-to-all(f32[16,32,256]{2,1,0:T(8,128)S(1)} %bitcast.86), channel_id=1, replica_groups={{0,2,4,6,8,10,12,14,16,18,20,22,24,26,28,30},{1,3,5,7,9,11,13,15,17,19,..., dimensions={0} | all-to-all | bytes 1048576 | tf_op jit(solution)/shard_map/all_to_all | solution.py:105
  31.2 0.2 fusion.25
  31.3 3.7 %collective-permute-start.1 = (f32[2,16,16]{2,1,0:T(8,128)S(1)}, f32[2,16,16]{2,1,0:T(8,128)S(1)}, u32[]{:S(2)}, u32[]{:S(2)}) collective-permute-start(f32[2,16,16]{2,1,0:T(8,128)S(1)} %fusion.25), channel_id=1, source_target_pairs={{0,1},{1,0},{2,3},{3,2},{4,5},{5,4},{6,7},{7,6},{8,9},{9,8},{10,11... | collective-permute-start | bytes 6152 | tf_op jit(solution)/shard_map/ppermute | solution.py:134
  35.0 0.8 collective-permute-done.1
  35.9 0.2 fusion.26
  36.0 0.8 broadcast_in_dim.21
  36.9 4.4 %all-to-all-start.1 = ((f32[16,32,256]{2,1,0:T(8,128)}), f32[16,32,256]{2,1,0:T(8,128)}, u32[]{:S(2)}, u32[]{:S(2)}) async-start(f32[16,32,256]{2,1,0:T(8,128)} %broadcast_in_dim.21), calls=%async_computation.1 | async-start | bytes 1048576 | tf_op jit(solution)/shard_map/all_to_all | solution.py:105
  41.3 0.3 pad_maximum_fusion
  41.5 0.3 copy.10
  41.9 13.6 %all-to-all-done.1 = f32[16,32,256]{2,1,0:T(8,128)} async-done(((f32[16,32,256]{2,1,0:T(8,128)}), f32[16,32,256]{2,1,0:T(8,128)}, u32[]{:S(2)}, u32[]{:S(2)}) %all-to-all-start.1) | async-done | bytes 524320 | tf_op jit(solution)/shard_map/all_to_all | solution.py:105
  55.5 2.0 fusion.27
  57.5 23.3 %all_to_all.51 = f32[8,64,256]{2,1,0:T(8,128)S(1)} all-to-all(f32[8,64,256]{2,1,0:T(8,128)S(1)} %fusion.27), channel_id=1, replica_groups={{0,32,64,96,128,160,192,224},{256,288,320,352,384,416,448,480},{1,33,65..., dimensions={0} | all-to-all | bytes 1048576 | tf_op jit(solution)/shard_map/all_to_all | solution.py:105
  80.8 4.8 %collective-permute-start.2 = (f32[64,256]{1,0:T(8,128)S(1)}, f32[64,256]{1,0:T(8,128)S(1)}, u32[]{:S(2)}, u32[]{:S(2)}) collective-permute-start(f32[64,256]{1,0:T(8,128)S(1)} %reduce_sum.46), channel_id=1, source_target_pairs={{0,256},{32,288},{64,320},{96,352},{128,384},{160,416},{192,448},{... | collective-permute-start | bytes 196616 | tf_op jit(solution)/shard_map/ppermute | solution.py:155
  85.6 4.2 %collective-permute-done.2 = f32[64,256]{1,0:T(8,128)S(1)} collective-permute-done((f32[64,256]{1,0:T(8,128)S(1)}, f32[64,256]{1,0:T(8,128)S(1)}, u32[]{:S(2)}, u32[]{:S(2)}) %collective-permute-start.2) | collective-permute-done | bytes 65568 | tf_op jit(solution)/shard_map/ppermute | solution.py:155
  89.8 15.6 %all_to_all.52 = f32[8,64,256]{2,1,0:T(8,128)S(1)} all-to-all(f32[8,64,256]{2,1,0:T(8,128)S(1)} %broadcast_in_dim.22), channel_id=1, replica_groups={{0,32,64,96,128,160,192,224},{256,288,320,352,384,416,448,480},{1,33,65..., dimensions={0} | all-to-all | bytes 1048576 | tf_op jit(solution)/shard_map/all_to_all | solution.py:105
  105.4 0.2 copy.11
  105.6 0.6 fusion.29
  106.2 1.0 fusion.28
  107.2 0.1 pad_maximum_fusion.1
  107.3 22.8 %all_to_all.53 = f32[16,48,256]{2,1,0:T(8,128)S(1)} all-to-all(f32[16,48,256]{2,1,0:T(8,128)S(1)} %pad_maximum_fusion.1), channel_id=1, replica_groups={{0,2,4,6,8,10,12,14,16,18,20,22,24,26,28,30},{1,3,5,7,9,11,13,15,17,19,..., dimensions={0} | all-to-all | bytes 1572864 | tf_op jit(solution)/shard_map/all_to_all | solution.py:105
  130.1 0.1 reduce_sum.47
  130.2 0.1 broadcast_in_dim.23
  130.3 26.0 %all_to_all.54 = f32[16,48,256]{2,1,0:T(8,128)S(1)} all-to-all(f32[16,48,256]{2,1,0:T(8,128)S(1)} %broadcast_in_dim.23), channel_id=1, replica_groups={{0,2,4,6,8,10,12,14,16,18,20,22,24,26,28,30},{1,3,5,7,9,11,13,15,17,19,..., dimensions={0} | all-to-all | bytes 1572864 | tf_op jit(solution)/shard_map/all_to_all | solution.py:105
  156.2 0.7 slice.43
  157.0 9.9 %shard_map.67 = f32[256,256]{1,0:T(8,128)} custom-call(f32[256,256]{1,0:T(8,128)} %bitcast.89), custom_call_target="tpu_custom_call" | custom-call | tf_op jit(solution)/shard_map/pallas_call | solution.py:96
  166.9 0.9 copy-done.3
  167.8 0.6 convolution_multiply_fusion.1
  168.4 0.6 fusion.30
  169.0 4.7 %collective-permute-start.3 = (f32[32,16,16]{2,1,0:T(8,128)S(1)}, f32[32,16,16]{2,1,0:T(8,128)S(1)}, u32[]{:S(2)}, u32[]{:S(2)}) collective-permute-start(f32[32,16,16]{2,1,0:T(8,128)S(1)} %fusion.30), channel_id=1, source_target_pairs={{0,1},{1,0},{2,3},{3,2},{4,5},{5,4},{6,7},{7,6},{8,9},{9,8},{10,11... | collective-permute-start | bytes 98312 | tf_op jit(solution)/shard_map/ppermute | solution.py:134
  173.8 1.1 collective-permute-done.3
  174.9 0.6 fusion.31
  175.5 1.0 fusion.32
  176.5 21.6 %all_to_all.55 = f32[8,64,256]{2,1,0:T(8,128)S(1)} all-to-all(f32[8,64,256]{2,1,0:T(8,128)S(1)} %fusion.32), channel_id=1, replica_groups={{0,32,64,96,128,160,192,224},{256,288,320,352,384,416,448,480},{1,33,65..., dimensions={0} | all-to-all | bytes 1048576 | tf_op jit(solution)/shard_map/all_to_all | solution.py:105
  198.1 4.8 %collective-permute-start.4 = (f32[64,256]{1,0:T(8,128)S(1)}, f32[64,256]{1,0:T(8,128)S(1)}, u32[]{:S(2)}, u32[]{:S(2)}) collective-permute-start(f32[64,256]{1,0:T(8,128)S(1)} %reduce_sum.48), channel_id=1, source_target_pairs={{0,256},{32,288},{64,320},{96,352},{128,384},{160,416},{192,448},{... | collective-permute-start | bytes 196616 | tf_op jit(solution)/shard_map/ppermute | solution.py:155
  202.9 4.2 %collective-permute-done.4 = f32[64,256]{1,0:T(8,128)S(1)} collective-permute-done((f32[64,256]{1,0:T(8,128)S(1)}, f32[64,256]{1,0:T(8,128)S(1)}, u32[]{:S(2)}, u32[]{:S(2)}) %collective-permute-start.4) | collective-permute-done | bytes 65568 | tf_op jit(solution)/shard_map/ppermute | solution.py:155
  207.1 16.2 %all_to_all.56 = f32[8,64,256]{2,1,0:T(8,128)S(1)} all-to-all(f32[8,64,256]{2,1,0:T(8,128)S(1)} %broadcast_in_dim.48), channel_id=1, replica_groups={{0,32,64,96,128,160,192,224},{256,288,320,352,384,416,448,480},{1,33,65..., dimensions={0} | all-to-all | bytes 1048576 | tf_op jit(solution)/shard_map/all_to_all | solution.py:105
  223.3 1.0 fusion.33
  224.3 0.2 copy.12
  224.5 0.6 fusion.34
  225.1 0.1 pad_maximum_fusion.2
  225.2 21.5 %all_to_all.57 = f32[16,48,256]{2,1,0:T(8,128)S(1)} all-to-all(f32[16,48,256]{2,1,0:T(8,128)S(1)} %pad_maximum_fusion.2), channel_id=1, replica_groups={{0,2,4,6,8,10,12,14,16,18,20,22,24,26,28,30},{1,3,5,7,9,11,13,15,17,19,..., dimensions={0} | all-to-all | bytes 1572864 | tf_op jit(solution)/shard_map/all_to_all | solution.py:105
  246.7 0.1 reduce_sum.49
  246.7 1.0 broadcast_in_dim.49
  247.7 5.3 %all-to-all-start.9 = ((f32[16,48,256]{2,1,0:T(8,128)}), f32[16,48,256]{2,1,0:T(8,128)S(1)}, u32[]{:S(2)}, u32[]{:S(2)}) async-start(f32[16,48,256]{2,1,0:T(8,128)} %broadcast_in_dim.49), calls=%async_computation.9 | async-start | bytes 1572864 | tf_op jit(solution)/shard_map/all_to_all | solution.py:105
  253.0 16.0 %all-to-all-done.9 = f32[16,48,256]{2,1,0:T(8,128)S(1)} async-done(((f32[16,48,256]{2,1,0:T(8,128)}), f32[16,48,256]{2,1,0:T(8,128)S(1)}, u32[]{:S(2)}, u32[]{:S(2)}) %all-to-all-start.9) | async-done | bytes 786464 | tf_op jit(solution)/shard_map/all_to_all | solution.py:105
  269.1 0.7 slice.45
  269.8 9.9 %shard_map.68 = f32[256,256]{1,0:T(8,128)} custom-call(f32[256,256]{1,0:T(8,128)} %bitcast.90), custom_call_target="tpu_custom_call" | custom-call | tf_op jit(solution)/shard_map/pallas_call | solution.py:96
  279.8 0.9 copy-done
  280.7 0.6 convolution_multiply_fusion
  281.3 0.4 fusion.35
  281.7 7.4 %collective-permute-start.6 = (f32[256,256]{1,0:T(8,128)S(1)}, f32[256,256]{1,0:T(8,128)S(1)}, u32[]{:S(2)}, u32[]{:S(2)}) collective-permute-start(f32[256,256]{1,0:T(8,128)S(1)} %fusion.35), channel_id=1, source_target_pairs={{0,1},{1,0},{2,3},{3,2},{4,5},{5,4},{6,7},{7,6},{8,9},{9,8},{10,11... | collective-permute-start | bytes 786440 | tf_op jit(solution)/shard_map/ppermute | solution.py:134
  289.1 1.9 collective-permute-start.5
  291.0 0.0 collective-permute-done.6
  291.1 1.2 broadcast_select_fusion.1
  292.3 0.6 collective-permute-done.5
  292.9 0.4 fusion.8
  293.2 1.4 fusion.4
  (25 shorter events, 0.4 us)
Async XLA Ops:
  0.6 10.5 %copy-start.4 = (f32[256,256]{1,0:T(8,128)S(1)}, f32[256,256]{1,0:T(8,128)}, u32[]{:S(2)}) copy-start(f32[256,256]{1,0:T(8,128)} %param.7) | copy-start | bytes 786436
  0.7 10.5 %copy-start.5 = (f32[256,256]{1,0:T(8,128)S(1)}, f32[256,256]{1,0:T(8,128)}, u32[]{:S(2)}) copy-start(f32[256,256]{1,0:T(8,128)} %param.6) | copy-start | bytes 786436
  0.7 10.6 %copy-start.2 = (f32[32,16,256]{2,1,0:T(8,128)S(1)}, f32[32,16,256]{2,1,0:T(8,128)}, u32[]{:S(2)}) copy-start(f32[32,16,256]{2,1,0:T(8,128)} %param.5) | copy-start | bytes 1572868
  2.2 9.0 %copy-start.1 = (f32[32,16,256]{2,1,0:T(8,128)S(1)}, f32[32,16,256]{2,1,0:T(8,128)}, u32[]{:S(2)}) copy-start(f32[32,16,256]{2,1,0:T(8,128)} %param.4) | copy-start | bytes 1572868
  2.2 10.8 %collective-permute-start = (f32[768,256]{1,0:T(8,128)S(1)}, f32[768,256]{1,0:T(8,128)S(1)}, u32[]{:S(2)}, u32[]{:S(2)}) collective-permute-start(f32[768,256]{1,0:T(8,128)S(1)} %maximum_select_fusion), channel_id=1, source_target_pairs={{0,1},{1,0},{2,3},{3,2},{4,5},{5,4},{6,7},{7,6},{8,9},{9,8},{10,11... | collective-permute-start | bytes 2359304 | tf_op jit(solution)/shard_map/ppermute | solution.py:134
  31.3 4.6 %collective-permute-start.1 = (f32[2,16,16]{2,1,0:T(8,128)S(1)}, f32[2,16,16]{2,1,0:T(8,128)S(1)}, u32[]{:S(2)}, u32[]{:S(2)}) collective-permute-start(f32[2,16,16]{2,1,0:T(8,128)S(1)} %fusion.25), channel_id=1, source_target_pairs={{0,1},{1,0},{2,3},{3,2},{4,5},{5,4},{6,7},{7,6},{8,9},{9,8},{10,11... | collective-permute-start | bytes 6152 | tf_op jit(solution)/shard_map/ppermute | solution.py:134
  36.9 18.6 %all-to-all-start.1 = ((f32[16,32,256]{2,1,0:T(8,128)}), f32[16,32,256]{2,1,0:T(8,128)}, u32[]{:S(2)}, u32[]{:S(2)}) async-start(f32[16,32,256]{2,1,0:T(8,128)} %broadcast_in_dim.21), calls=%async_computation.1 | async-start | bytes 1048576 | tf_op jit(solution)/shard_map/all_to_all | solution.py:105
  80.8 8.9 %collective-permute-start.2 = (f32[64,256]{1,0:T(8,128)S(1)}, f32[64,256]{1,0:T(8,128)S(1)}, u32[]{:S(2)}, u32[]{:S(2)}) collective-permute-start(f32[64,256]{1,0:T(8,128)S(1)} %reduce_sum.46), channel_id=1, source_target_pairs={{0,256},{32,288},{64,320},{96,352},{128,384},{160,416},{192,448},{... | collective-permute-start | bytes 196616 | tf_op jit(solution)/shard_map/ppermute | solution.py:155
  166.9 0.9 copy-start.3
  169.0 5.9 %collective-permute-start.3 = (f32[32,16,16]{2,1,0:T(8,128)S(1)}, f32[32,16,16]{2,1,0:T(8,128)S(1)}, u32[]{:S(2)}, u32[]{:S(2)}) collective-permute-start(f32[32,16,16]{2,1,0:T(8,128)S(1)} %fusion.30), channel_id=1, source_target_pairs={{0,1},{1,0},{2,3},{3,2},{4,5},{5,4},{6,7},{7,6},{8,9},{9,8},{10,11... | collective-permute-start | bytes 98312 | tf_op jit(solution)/shard_map/ppermute | solution.py:134
  198.1 8.9 %collective-permute-start.4 = (f32[64,256]{1,0:T(8,128)S(1)}, f32[64,256]{1,0:T(8,128)S(1)}, u32[]{:S(2)}, u32[]{:S(2)}) collective-permute-start(f32[64,256]{1,0:T(8,128)S(1)} %reduce_sum.48), channel_id=1, source_target_pairs={{0,256},{32,288},{64,320},{96,352},{128,384},{160,416},{192,448},{... | collective-permute-start | bytes 196616 | tf_op jit(solution)/shard_map/ppermute | solution.py:155
  247.7 21.4 %all-to-all-start.9 = ((f32[16,48,256]{2,1,0:T(8,128)}), f32[16,48,256]{2,1,0:T(8,128)S(1)}, u32[]{:S(2)}, u32[]{:S(2)}) async-start(f32[16,48,256]{2,1,0:T(8,128)} %broadcast_in_dim.49), calls=%async_computation.9 | async-start | bytes 1572864 | tf_op jit(solution)/shard_map/all_to_all | solution.py:105
  279.7 0.9 copy-start
  281.7 9.3 %collective-permute-start.6 = (f32[256,256]{1,0:T(8,128)S(1)}, f32[256,256]{1,0:T(8,128)S(1)}, u32[]{:S(2)}, u32[]{:S(2)}) collective-permute-start(f32[256,256]{1,0:T(8,128)S(1)} %fusion.35), channel_id=1, source_target_pairs={{0,1},{1,0},{2,3},{3,2},{4,5},{5,4},{6,7},{7,6},{8,9},{9,8},{10,11... | collective-permute-start | bytes 786440 | tf_op jit(solution)/shard_map/ppermute | solution.py:134
  289.1 3.8 %collective-permute-start.5 = (f32[512,256]{1,0:T(8,128)S(1)}, f32[512,256]{1,0:T(8,128)S(1)}, u32[]{:S(2)}, u32[]{:S(2)}) collective-permute-start(f32[512,256]{1,0:T(8,128)S(1)} %convolution_multiply_fusion), channel_id=1, source_target_pairs={{0,1},{1,0},{2,3},{3,2},{4,5},{5,4},{6,7},{7,6},{8,9},{9,8},{10,11... | collective-permute-start | bytes 1572872 | tf_op jit(solution)/shard_map/ppermute | solution.py:134

commit v4 on v3

--- a/solution.py
+++ b/solution.py
@@ -15,6 +15,7 @@
 BF16 = jnp.bfloat16
 LANES = 128
 PANEL = 8
+VMEM_BYTES = 32 * 1024 * 1024
 
 
 def mm(a, b, ca, cb):
@@ -36,9 +37,8 @@
     return a1, a2, rest - a2
 
 
-def inverse_factor_kernel(gram_ref, x_ref):
-    n = gram_ref.shape[-1]
-    x_ref[...] = gram_ref[...] * (1.0 / PROJ_WIDTH)
+def invert_factor(x_ref):
+    n = x_ref.shape[-1]
     lane = lax.broadcasted_iota(jnp.int32, (PANEL, n), 1)
     sub = lax.broadcasted_iota(jnp.int32, (PANEL, n), 0)
     widen = lambda v: jnp.concatenate([v] * (n // LANES), 1)
@@ -92,13 +92,80 @@
     x_ref[...] = jnp.where(col <= row, x_ref[...], 0.0)
 
 
-def inverse_factor(gram):
+def project_kernel(w_ref, raw_ref, out_ref):
+    chips = out_ref.shape[0]
+    rows = w_ref.shape[0] // chips
+    raw = raw_ref[...]
+    y = mm(w_ref[...], raw, 1, 0)
+    for i in range(chips):
+        for h in range(2):
+            out_ref[i, h * rows:(h + 1) * rows, :] = (
+                y[i * rows:(i + 1) * rows, h * LANES:(h + 1) * LANES]
+            )
+    top = mm(raw[:, :LANES], raw, 0, 0)
+    low = mm(raw[:, LANES:], raw[:, LANES:], 0, 0)
+    per_chip = 3 * LANES // chips
+    for j, block in enumerate((top[:, :LANES], top[:, LANES:], low)):
+        for k in range(0, LANES, 8):
+            at = j * LANES + k
+            i, off = at // per_chip, at % per_chip + 2 * rows
+            out_ref[i, off:off + 8, :] = block[k:k + 8, :]
+
+
+def project(w, raw, chips):
+    rows = 2 * w.shape[0] // chips + 3 * LANES // chips
     return pl.pallas_call(
-        inverse_factor_kernel,
-        out_shape=jax.ShapeDtypeStruct(gram.shape, F32),
-        in_specs=[pl.BlockSpec(memory_space=pltpu.VMEM)],
+        project_kernel,
+        out_shape=jax.ShapeDtypeStruct((chips, rows, LANES), F32),
+        in_specs=[pl.BlockSpec(memory_space=pltpu.VMEM)] * 2,
         out_specs=pl.BlockSpec(memory_space=pltpu.VMEM),
-    )(gram)
+        compiler_params=pltpu.CompilerParams(vmem_limit_bytes=VMEM_BYTES),
+    )(w, raw)
+
+
+def factor_and_project(whole_ref, x_ref, y_ref):
+    chips = whole_ref.shape[0]
+    rows = y_ref.shape[0] // chips
+    per_chip = 3 * LANES // chips
+    for i in range(chips):
+        for h in range(2):
+            y_ref[i * rows:(i + 1) * rows, h * LANES:(h + 1) * LANES] = (
+                whole_ref[i, h * rows:(h + 1) * rows, :]
+            )
+    x_ref[LANES:, :LANES] = jnp.zeros((LANES, LANES), F32)
+    for j, (top, left) in enumerate(((0, 0), (0, LANES), (LANES, LANES))):
+        for k in range(0, LANES, 8):
+            at = j * LANES + k
+            i, off = at // per_chip, at % per_chip + 2 * rows
+            x_ref[top + k:top + k + 8, left:left + LANES] = (
+                whole_ref[i, off:off + 8, :] * (1.0 / PROJ_WIDTH)
+            )
+    invert_factor(x_ref)
+    return mm(y_ref[...], x_ref[...], 1, 1) * (1.0 / math.sqrt(PROJ_WIDTH))
+
+
+def middle_kernel(whole_ref, p_ref, x_ref, y_ref):
+    p_ref[...] = factor_and_project(whole_ref, x_ref, y_ref)
+
+
+def last_kernel(whole_ref, raw_ref, sent_ref, here_ref, x_ref, y_ref):
+    n = y_ref.shape[0]
+    half = here_ref.shape[0]
+    sent_ref[:n, :] = factor_and_project(whole_ref, x_ref, y_ref)
+    basis = mm(raw_ref[...], x_ref[...], 1, 1)
+    here_ref[...] = basis[:half, :]
+    sent_ref[n:, :] = basis[half:, :]
+
+
+def call_on_whole(kernel, outs, n, r, *args):
+    return pl.pallas_call(
+        kernel,
+        out_shape=[jax.ShapeDtypeStruct((rows, r), F32) for rows in outs],
+        in_specs=[pl.BlockSpec(memory_space=pltpu.VMEM)] * len(args),
+        out_specs=[pl.BlockSpec(memory_space=pltpu.VMEM)] * len(outs),
+        scratch_shapes=[pltpu.VMEM((r, r), F32), pltpu.VMEM((n, r), F32)],
+        compiler_params=pltpu.CompilerParams(vmem_limit_bytes=VMEM_BYTES),
+    )(*args)
 
 
 def exchange(chunks, axis, groups):
@@ -154,19 +221,16 @@
         own = scatter_sum(part.reshape(n_z, 2 * feats // n_z, r), "tenant", along_z)
         own = own + lax.ppermute(own, "tenant", swap_halves)
         raw = gather(own, "tenant", along_z).reshape(2 * feats, r)
-        partial = mm(w, raw, 1, 0).reshape(chips, mine * rank, r)
-        gram = mm(raw, raw, 0, 0).reshape(chips, r // chips, r)
-        own = scatter_sum(jnp.concatenate([partial, gram], 1), "feat", same_core)
+        own = scatter_sum(project(w, raw, chips), "feat", same_core)
         whole = gather(own, "feat", same_core)
-        x = inverse_factor(whole[:, mine * rank:].reshape(r, r))
-        p = mm(whole[:, :mine * rank].reshape(tenants * rank, r), x, 1, 1) * root
+        n = tenants * rank
         if step < ITERS - 1:
-            p = p.reshape(tenants, rank, r)
+            p = call_on_whole(middle_kernel, [n], n, r, whole)[0].reshape(tenants, rank, r)
             other_gram = to_partner(bmm(p, p, 2, 2))
-            factor = bmm(other_gram, p, 2, 1).reshape(tenants * rank, r)
-    other = to_partner(p)
-    away = to_partner(mm(raw[feats:], x, 1, 1))
-    here = mm(raw[:feats], x, 1, 1)
+            factor = bmm(other_gram, p, 2, 1).reshape(n, r)
+    sent, here = call_on_whole(last_kernel, [n + feats, feats], n, r, whole, raw)
+    got = to_partner(sent)
+    p, other, away = sent[:n], got[:n], got[n:]
     n_rows = r // n_feat
     first = lax.axis_index("feat") * n_rows
     one_hot = lax.broadcasted_iota(jnp.int32, (n_rows, r), 1) == (

time: 296 us -> 281 us (0.949)
  blocking collectives: 164 us -> 184 us
  waiting for transfers between devices: 42.2 us -> 27.4 us
  starting transfers between devices: 45.9 us -> 35.5 us
  matrix products: 13.2 us -> 7.18 us
  local copies, waits for them, and re-layouts: 6.13 us -> 1.42 us
    all_to_all x8 -> x9, blocking collectives: 164 us -> 184 us  [exchange(): lax.all_to_all(chunks, axis, 0, 0, tiled=True, axis_index_groups=groups)]
    all_to_all x2 -> x1, waiting for transfers between devices: 29.6 us -> 13.6 us  [exchange(): lax.all_to_all(chunks, axis, 0, 0, tiled=True, axis_index_groups=groups)]
    dot_general x13 -> x5, matrix products: 11.7 us -> 5.7 us  [mm(): lax.dot_general(a, b, (((ca,), (cb,)), ((), ())), precision=HIGH_PRECISIO...]
    all_to_all x2 -> x1, starting transfers between devices: 9.68 us -> 4.37 us  [exchange(): lax.all_to_all(chunks, axis, 0, 0, tiled=True, axis_index_groups=groups)]
    ppermute x5 -> x4, starting transfers between devices: 26.7 us -> 21.7 us  [to_partner(): return lax.ppermute(x, 'feat', swap_cores)]
    pallas_call x2 -> x4, Pallas kernels: 19.8 us -> 20.8 us  [the longest x2 17.9 us: call_on_whole(): pl.pallas_call(kernel, out_shape=[jax.ShapeDtypeStruct((rows, r), F32) fo...]
  transfers between devices with their start and end apart: 9 -> 7, of which waited for: 8 -> 7; matrix products, arithmetic and copies ran while one was open for 1% -> 0% of each run, Pallas kernels for 0% -> 0%
where the time goes in v4:
time: 281 us
  blocking collectives  184 us (65%)
  starting transfers between devices  35.5 us (13%)
  waiting for transfers between devices  27.4 us (10%)
  Pallas kernels  20.8 us (7%)
  matrix products  7.18 us (3%)
  other arithmetic  2.97 us (1%)
    all_to_all x9, blocking collectives, exchange(): lax.all_to_all(chunks, axis, 0, 0, tiled=True, axis_index_groups=groups)  184 us
    ppermute x4, starting transfers between devices, to_partner(): return lax.ppermute(x, 'feat', swap_cores)  21.7 us
    pallas_call x2, Pallas kernels, call_on_whole(): pl.pallas_call(kernel, out_shape=[jax.ShapeDtypeStruct((rows, r), F32) fo...  17.9 us
    all_to_all x1, waiting for transfers between devices, exchange(): lax.all_to_all(chunks, axis, 0, 0, tiled=True, axis_index_groups=groups)  13.6 us
    ppermute x2, starting transfers between devices, body(): own = own + lax.ppermute(own, 'tenant', swap_halves)  9.51 us
    ppermute x2, waiting for transfers between devices, body(): own = own + lax.ppermute(own, 'tenant', swap_halves)  8.31 us
    dot_general x5, matrix products, mm(): lax.dot_general(a, b, (((ca,), (cb,)), ((), ())), precision=HIGH_PRECISIO...  5.7 us
  transfers between devices with their start and end apart: 7, of which 7 were waited for; matrix products, arithmetic and copies ran while one was open for 0% of the time, Pallas kernels for 0%

profile of v4, /device:TPU:1, one launch (start us, length us, event | category | flops | bytes accessed | tf_op | source)
XLA Modules:
  0.0 280.5 jit_solution(11901471193781043896)
XLA Ops:
  0.6 0.0 copy-start.2
  0.7 0.0 copy-start.3
  0.7 0.0 copy-start.1
  0.7 1.5 maximum_select_fusion
  2.2 0.0 copy-start
  2.2 8.9 %collective-permute-start = (f32[768,256]{1,0:T(8,128)S(1)}, f32[768,256]{1,0:T(8,128)S(1)}, u32[]{:S(2)}, u32[]{:S(2)}) collective-permute-start(f32[768,256]{1,0:T(8,128)S(1)} %maximum_select_fusion), channel_id=1, source_target_pairs={{0,1},{1,0},{2,3},{3,2},{4,5},{5,4},{6,7},{7,6},{8,9},{9,8},{10,11... | collective-permute-start | bytes 2359304 | tf_op jit(solution)/shard_map/ppermute | solution.py:201
  11.2 0.0 copy-done.2
  11.2 0.0 copy-done.3
  11.2 0.0 copy-done.1
  11.2 0.0 copy-done
  11.2 0.1 broadcast_select_fusion
  11.3 1.7 collective-permute-done
  13.1 1.0 fusion
  14.1 17.0 %all_to_all.50 = f32[16,32,256]{2,1,0:T(8,128)S(1)} all-to-all(f32[16,32,256]{2,1,0:T(8,128)S(1)} %bitcast.44), channel_id=1, replica_groups={{0,2,4,6,8,10,12,14,16,18,20,22,24,26,28,30},{1,3,5,7,9,11,13,15,17,19,..., dimensions={0} | all-to-all | bytes 1048576 | tf_op jit(solution)/shard_map/all_to_all | solution.py:172
  31.2 0.2 fusion.28
  31.3 3.7 %collective-permute-start.1 = (f32[2,16,16]{2,1,0:T(8,128)S(1)}, f32[2,16,16]{2,1,0:T(8,128)S(1)}, u32[]{:S(2)}, u32[]{:S(2)}) collective-permute-start(f32[2,16,16]{2,1,0:T(8,128)S(1)} %fusion.28), channel_id=1, source_target_pairs={{0,1},{1,0},{2,3},{3,2},{4,5},{5,4},{6,7},{7,6},{8,9},{9,8},{10,11... | collective-permute-start | bytes 6152 | tf_op jit(solution)/shard_map/ppermute | solution.py:201
  35.0 0.8 collective-permute-done.1
  35.9 0.2 fusion.29
  36.0 0.8 broadcast_in_dim.21
  36.9 4.4 %all-to-all-start.1 = ((f32[16,32,256]{2,1,0:T(8,128)}), f32[16,32,256]{2,1,0:T(8,128)}, u32[]{:S(2)}, u32[]{:S(2)}) async-start(f32[16,32,256]{2,1,0:T(8,128)} %broadcast_in_dim.21), calls=%async_computation.1 | async-start | bytes 1048576 | tf_op jit(solution)/shard_map/all_to_all | solution.py:172
  41.3 0.3 fusion.27
  41.5 0.3 copy.9
  41.9 13.6 %all-to-all-done.1 = f32[16,32,256]{2,1,0:T(8,128)} async-done(((f32[16,32,256]{2,1,0:T(8,128)}), f32[16,32,256]{2,1,0:T(8,128)}, u32[]{:S(2)}, u32[]{:S(2)}) %all-to-all-start.1) | async-done | bytes 524320 | tf_op jit(solution)/shard_map/all_to_all | solution.py:172
  55.5 2.0 fusion.30
  57.5 23.3 %all_to_all.51 = f32[8,64,256]{2,1,0:T(8,128)S(1)} all-to-all(f32[8,64,256]{2,1,0:T(8,128)S(1)} %fusion.30), channel_id=1, replica_groups={{0,32,64,96,128,160,192,224},{256,288,320,352,384,416,448,480},{1,33,65..., dimensions={0} | all-to-all | bytes 1048576 | tf_op jit(solution)/shard_map/all_to_all | solution.py:172
  80.8 4.8 %collective-permute-start.2 = (f32[64,256]{1,0:T(8,128)S(1)}, f32[64,256]{1,0:T(8,128)S(1)}, u32[]{:S(2)}, u32[]{:S(2)}) collective-permute-start(f32[64,256]{1,0:T(8,128)S(1)} %reduce_sum.46), channel_id=1, source_target_pairs={{0,256},{32,288},{64,320},{96,352},{128,384},{160,416},{192,448},{... | collective-permute-start | bytes 196616 | tf_op jit(solution)/shard_map/ppermute | solution.py:222
  85.6 4.2 %collective-permute-done.2 = f32[64,256]{1,0:T(8,128)S(1)} collective-permute-done((f32[64,256]{1,0:T(8,128)S(1)}, f32[64,256]{1,0:T(8,128)S(1)}, u32[]{:S(2)}, u32[]{:S(2)}) %collective-permute-start.2) | collective-permute-done | bytes 65568 | tf_op jit(solution)/shard_map/ppermute | solution.py:222
  89.8 15.6 %all_to_all.52 = f32[8,64,256]{2,1,0:T(8,128)S(1)} all-to-all(f32[8,64,256]{2,1,0:T(8,128)S(1)} %broadcast_in_dim.22), channel_id=1, replica_groups={{0,32,64,96,128,160,192,224},{256,288,320,352,384,416,448,480},{1,33,65..., dimensions={0} | all-to-all | bytes 1048576 | tf_op jit(solution)/shard_map/all_to_all | solution.py:172
  105.4 1.4 shard_map.67
  106.8 21.8 %all_to_all.53 = f32[16,88,128]{2,1,0:T(8,128)S(1)} all-to-all(f32[16,88,128]{2,1,0:T(8,128)S(1)} %shard_map.67), channel_id=1, replica_groups={{0,2,4,6,8,10,12,14,16,18,20,22,24,26,28,30},{1,3,5,7,9,11,13,15,17,19,..., dimensions={0} | all-to-all | bytes 1441792 | tf_op jit(solution)/shard_map/all_to_all | solution.py:172
  128.8 24.3 %all_to_all.54.whole_ref = f32[16,88,128]{2,1,0:T(8,128)S(1)} all-to-all(f32[16,88,128]{2,1,0:T(8,128)S(1)} %broadcast_in_dim.23), channel_id=1, replica_groups={{0,2,4,6,8,10,12,14,16,18,20,22,24,26,28,30},{1,3,5,7,9,11,13,15,17,19,..., dimensions={0} | all-to-all | bytes 1441792 | tf_op jit(solution)/shard_map/all_to_all | solution.py:172
  153.1 8.8 %shard_map.68 = f32[512,256]{1,0:T(8,128)S(1)} custom-call(f32[16,88,128]{2,1,0:T(8,128)S(1)} %all_to_all.54.whole_ref), custom_call_target="tpu_custom_call" | custom-call | tf_op jit(solution)/shard_map/pallas_call | solution.py:161
  161.8 0.6 fusion.31
  162.4 4.5 %collective-permute-start.3 = (f32[32,16,16]{2,1,0:T(8,128)S(1)}, f32[32,16,16]{2,1,0:T(8,128)S(1)}, u32[]{:S(2)}, u32[]{:S(2)}) collective-permute-start(f32[32,16,16]{2,1,0:T(8,128)S(1)} %fusion.31), channel_id=1, source_target_pairs={{0,1},{1,0},{2,3},{3,2},{4,5},{5,4},{6,7},{7,6},{8,9},{9,8},{10,11... | collective-permute-start | bytes 98312 | tf_op jit(solution)/shard_map/ppermute | solution.py:201
  167.0 1.1 collective-permute-done.3
  168.1 0.6 fusion.32
  168.7 1.0 fusion.33
  169.7 21.9 %all_to_all.55 = f32[8,64,256]{2,1,0:T(8,128)S(1)} all-to-all(f32[8,64,256]{2,1,0:T(8,128)S(1)} %fusion.33), channel_id=1, replica_groups={{0,32,64,96,128,160,192,224},{256,288,320,352,384,416,448,480},{1,33,65..., dimensions={0} | all-to-all | bytes 1048576 | tf_op jit(solution)/shard_map/all_to_all | solution.py:172
  191.6 4.8 %collective-permute-start.4 = (f32[64,256]{1,0:T(8,128)S(1)}, f32[64,256]{1,0:T(8,128)S(1)}, u32[]{:S(2)}, u32[]{:S(2)}) collective-permute-start(f32[64,256]{1,0:T(8,128)S(1)} %reduce_sum.48), channel_id=1, source_target_pairs={{0,256},{32,288},{64,320},{96,352},{128,384},{160,416},{192,448},{... | collective-permute-start | bytes 196616 | tf_op jit(solution)/shard_map/ppermute | solution.py:222
  196.4 4.2 %collective-permute-done.4 = f32[64,256]{1,0:T(8,128)S(1)} collective-permute-done((f32[64,256]{1,0:T(8,128)S(1)}, f32[64,256]{1,0:T(8,128)S(1)}, u32[]{:S(2)}, u32[]{:S(2)}) %collective-permute-start.4) | collective-permute-done | bytes 65568 | tf_op jit(solution)/shard_map/ppermute | solution.py:222
  200.6 16.3 %all_to_all.56 = f32[8,64,256]{2,1,0:T(8,128)S(1)} all-to-all(f32[8,64,256]{2,1,0:T(8,128)S(1)} %broadcast_in_dim.48), channel_id=1, replica_groups={{0,32,64,96,128,160,192,224},{256,288,320,352,384,416,448,480},{1,33,65..., dimensions={0} | all-to-all | bytes 1048576 | tf_op jit(solution)/shard_map/all_to_all | solution.py:172
  216.9 1.4 shard_map.69
  218.3 19.7 %all_to_all.57 = f32[16,88,128]{2,1,0:T(8,128)S(1)} all-to-all(f32[16,88,128]{2,1,0:T(8,128)S(1)} %shard_map.69), channel_id=1, replica_groups={{0,2,4,6,8,10,12,14,16,18,20,22,24,26,28,30},{1,3,5,7,9,11,13,15,17,19,..., dimensions={0} | all-to-all | bytes 1441792 | tf_op jit(solution)/shard_map/all_to_all | solution.py:172
  238.1 24.3 %all_to_all.58.whole_ref = f32[16,88,128]{2,1,0:T(8,128)S(1)} all-to-all(f32[16,88,128]{2,1,0:T(8,128)S(1)} %broadcast_in_dim.49), channel_id=1, replica_groups={{0,2,4,6,8,10,12,14,16,18,20,22,24,26,28,30},{1,3,5,7,9,11,13,15,17,19,..., dimensions={0} | all-to-all | bytes 1441792 | tf_op jit(solution)/shard_map/all_to_all | solution.py:172
  262.4 9.2 %shard_map.70 = (f32[768,256]{1,0:T(8,128)S(1)}, f32[256,256]{1,0:T(8,128)S(1)}) custom-call(f32[16,88,128]{2,1,0:T(8,128)S(1)} %all_to_all.58.whole_ref, f32[512,256]{1,0:T(8,128)S(1)} %bitcast.37), custom_call_target="tpu_custom_call" | custom-call | tf_op jit(solution)/shard_map/pallas_call | solution.py:161
  271.6 4.5 %collective-permute-start.5 = (f32[768,256]{1,0:T(8,128)S(1)}, f32[768,256]{1,0:T(8,128)S(1)}, u32[]{:S(2)}, u32[]{:S(2)}) collective-permute-start(f32[768,256]{1,0:T(8,128)S(1)} %get-tuple-element.5), channel_id=1, source_target_pairs={{0,1},{1,0},{2,3},{3,2},{4,5},{5,4},{6,7},{7,6},{8,9},{9,8},{10,11... | collective-permute-start | bytes 2359304 | tf_op jit(solution)/shard_map/ppermute | solution.py:201
  276.1 1.9 collective-permute-done.5
  278.0 0.8 slice_select_fusion
  278.8 0.4 fusion.8
  279.2 1.4 fusion.4
  (18 shorter events, 0.5 us)
Async XLA Ops:
  0.6 10.5 %copy-start.2 = (f32[256,256]{1,0:T(8,128)S(1)}, f32[256,256]{1,0:T(8,128)}, u32[]{:S(2)}) copy-start(f32[256,256]{1,0:T(8,128)} %param.7) | copy-start | bytes 786436
  0.7 10.5 %copy-start.3 = (f32[256,256]{1,0:T(8,128)S(1)}, f32[256,256]{1,0:T(8,128)}, u32[]{:S(2)}) copy-start(f32[256,256]{1,0:T(8,128)} %param.6) | copy-start | bytes 786436
  0.7 10.6 %copy-start.1 = (f32[32,16,256]{2,1,0:T(8,128)S(1)}, f32[32,16,256]{2,1,0:T(8,128)}, u32[]{:S(2)}) copy-start(f32[32,16,256]{2,1,0:T(8,128)} %param.5) | copy-start | bytes 1572868
  2.2 9.0 %copy-start = (f32[32,16,256]{2,1,0:T(8,128)S(1)}, f32[32,16,256]{2,1,0:T(8,128)}, u32[]{:S(2)}) copy-start(f32[32,16,256]{2,1,0:T(8,128)} %param.4) | copy-start | bytes 1572868
  2.2 10.8 %collective-permute-start = (f32[768,256]{1,0:T(8,128)S(1)}, f32[768,256]{1,0:T(8,128)S(1)}, u32[]{:S(2)}, u32[]{:S(2)}) collective-permute-start(f32[768,256]{1,0:T(8,128)S(1)} %maximum_select_fusion), channel_id=1, source_target_pairs={{0,1},{1,0},{2,3},{3,2},{4,5},{5,4},{6,7},{7,6},{8,9},{9,8},{10,11... | collective-permute-start | bytes 2359304 | tf_op jit(solution)/shard_map/ppermute | solution.py:201
  31.3 4.6 %collective-permute-start.1 = (f32[2,16,16]{2,1,0:T(8,128)S(1)}, f32[2,16,16]{2,1,0:T(8,128)S(1)}, u32[]{:S(2)}, u32[]{:S(2)}) collective-permute-start(f32[2,16,16]{2,1,0:T(8,128)S(1)} %fusion.28), channel_id=1, source_target_pairs={{0,1},{1,0},{2,3},{3,2},{4,5},{5,4},{6,7},{7,6},{8,9},{9,8},{10,11... | collective-permute-start | bytes 6152 | tf_op jit(solution)/shard_map/ppermute | solution.py:201
  36.9 18.6 %all-to-all-start.1 = ((f32[16,32,256]{2,1,0:T(8,128)}), f32[16,32,256]{2,1,0:T(8,128)}, u32[]{:S(2)}, u32[]{:S(2)}) async-start(f32[16,32,256]{2,1,0:T(8,128)} %broadcast_in_dim.21), calls=%async_computation.1 | async-start | bytes 1048576 | tf_op jit(solution)/shard_map/all_to_all | solution.py:172
  80.8 8.9 %collective-permute-start.2 = (f32[64,256]{1,0:T(8,128)S(1)}, f32[64,256]{1,0:T(8,128)S(1)}, u32[]{:S(2)}, u32[]{:S(2)}) collective-permute-start(f32[64,256]{1,0:T(8,128)S(1)} %reduce_sum.46), channel_id=1, source_target_pairs={{0,256},{32,288},{64,320},{96,352},{128,384},{160,416},{192,448},{... | collective-permute-start | bytes 196616 | tf_op jit(solution)/shard_map/ppermute | solution.py:222
  162.4 5.7 %collective-permute-start.3 = (f32[32,16,16]{2,1,0:T(8,128)S(1)}, f32[32,16,16]{2,1,0:T(8,128)S(1)}, u32[]{:S(2)}, u32[]{:S(2)}) collective-permute-start(f32[32,16,16]{2,1,0:T(8,128)S(1)} %fusion.31), channel_id=1, source_target_pairs={{0,1},{1,0},{2,3},{3,2},{4,5},{5,4},{6,7},{7,6},{8,9},{9,8},{10,11... | collective-permute-start | bytes 98312 | tf_op jit(solution)/shard_map/ppermute | solution.py:201
  191.6 8.9 %collective-permute-start.4 = (f32[64,256]{1,0:T(8,128)S(1)}, f32[64,256]{1,0:T(8,128)S(1)}, u32[]{:S(2)}, u32[]{:S(2)}) collective-permute-start(f32[64,256]{1,0:T(8,128)S(1)} %reduce_sum.48), channel_id=1, source_target_pairs={{0,256},{32,288},{64,320},{96,352},{128,384},{160,416},{192,448},{... | collective-permute-start | bytes 196616 | tf_op jit(solution)/shard_map/ppermute | solution.py:222
  271.6 6.4 %collective-permute-start.5 = (f32[768,256]{1,0:T(8,128)S(1)}, f32[768,256]{1,0:T(8,128)S(1)}, u32[]{:S(2)}, u32[]{:S(2)}) collective-permute-start(f32[768,256]{1,0:T(8,128)S(1)} %get-tuple-element.5), channel_id=1, source_target_pairs={{0,1},{1,0},{2,3},{3,2},{4,5},{5,4},{6,7},{7,6},{8,9},{9,8},{10,11... | collective-permute-start | bytes 2359304 | tf_op jit(solution)/shard_map/ppermute | solution.py:201

commit v5 on v4

--- a/solution.py
+++ b/solution.py
@@ -21,12 +21,6 @@
 def mm(a, b, ca, cb):
     return lax.dot_general(
         a, b, (((ca,), (cb,)), ((), ())), precision=HIGH_PRECISION, preferred_element_type=F32
-    )
-
-
-def bmm(a, b, ca, cb):
-    return lax.dot_general(
-        a, b, (((ca,), (cb,)), ((0,), (0,))), precision=HIGH_PRECISION, preferred_element_type=F32
     )
 
 
@@ -94,12 +88,14 @@
 
 def project_kernel(w_ref, raw_ref, out_ref):
     chips = out_ref.shape[0]
+    side = math.isqrt(chips)
+    chip_of = lambda b: b % side * side + b // side
     rows = w_ref.shape[0] // chips
     raw = raw_ref[...]
     y = mm(w_ref[...], raw, 1, 0)
     for i in range(chips):
         for h in range(2):
-            out_ref[i, h * rows:(h + 1) * rows, :] = (
+            out_ref[chip_of(i), h * rows:(h + 1) * rows, :] = (
                 y[i * rows:(i + 1) * rows, h * LANES:(h + 1) * LANES]
             )
     top = mm(raw[:, :LANES], raw, 0, 0)
@@ -109,18 +105,7 @@
         for k in range(0, LANES, 8):
             at = j * LANES + k
             i, off = at // per_chip, at % per_chip + 2 * rows
-            out_ref[i, off:off + 8, :] = block[k:k + 8, :]
-
-
-def project(w, raw, chips):
-    rows = 2 * w.shape[0] // chips + 3 * LANES // chips
-    return pl.pallas_call(
-        project_kernel,
-        out_shape=jax.ShapeDtypeStruct((chips, rows, LANES), F32),
-        in_specs=[pl.BlockSpec(memory_space=pltpu.VMEM)] * 2,
-        out_specs=pl.BlockSpec(memory_space=pltpu.VMEM),
-        compiler_params=pltpu.CompilerParams(vmem_limit_bytes=VMEM_BYTES),
-    )(w, raw)
+            out_ref[chip_of(i), off:off + 8, :] = block[k:k + 8, :]
 
 
 def factor_and_project(whole_ref, x_ref, y_ref):
@@ -144,8 +129,78 @@
     return mm(y_ref[...], x_ref[...], 1, 1) * (1.0 / math.sqrt(PROJ_WIDTH))
 
 
-def middle_kernel(whole_ref, p_ref, x_ref, y_ref):
-    p_ref[...] = factor_and_project(whole_ref, x_ref, y_ref)
+def same_block(shape, row_block, col_block):
+    return (
+        lax.broadcasted_iota(jnp.int32, shape, 0) // row_block
+        == lax.broadcasted_iota(jnp.int32, shape, 1) // col_block
+    )
+
+
+def first_gram_kernel(rank, parts_ref, p_ref, gram_ref):
+    p = jnp.sum(parts_ref[...], 0) * (1.0 / math.sqrt(PROJ_WIDTH))
+    p_ref[...] = p
+    gram = mm(p, p, 1, 1)
+    gram_ref[...] = jnp.where(same_block(gram.shape, rank, rank), gram, 0.0)
+
+
+def first_factor_kernel(p_ref, gram_ref, out_ref):
+    factor = mm(gram_ref[...], p_ref[...], 1, 0)
+    for i in range(out_ref.shape[0]):
+        out_ref[i] = factor
+
+
+def middle_kernel(rank, whole_ref, p_ref, gram_ref, x_ref, y_ref):
+    p = factor_and_project(whole_ref, x_ref, y_ref)
+    p_ref[...] = p
+    for k in range(0, p.shape[0], LANES):
+        gram = mm(p[k:k + LANES], p[k:k + LANES], 1, 1)
+        gram = jnp.where(same_block(gram.shape, rank, rank), gram, 0.0)
+        packed = gram[:rank]
+        for i in range(rank, LANES, rank):
+            packed = packed + gram[i:i + rank]
+        gram_ref[:, k:k + LANES] = packed
+
+
+def first_update_kernel(w_ref, factor_ref, part_ref):
+    part_ref[...] = mm(w_ref[...], factor_ref[...], 0, 0)
+
+
+def update_kernel(gram_ref, p_ref, w_ref, part_ref, f_ref):
+    rank = gram_ref.shape[0]
+    for k in range(0, f_ref.shape[0], LANES):
+        gram = jnp.concatenate([gram_ref[:, k:k + LANES]] * (LANES // rank), 0)
+        gram = jnp.where(same_block(gram.shape, rank, rank), gram, 0.0)
+        f_ref[k:k + LANES, :] = mm(gram, p_ref[k:k + LANES, :], 1, 0)
+    part_ref[...] = mm(w_ref[...], f_ref[...], 0, 0)
+
+
+def cores_kernel(rank, n_rows, at_ref, sent_ref, got_ref, here_ref, cores_ref, out_ref, in_ref):
+    n = sent_ref.shape[0] - here_ref.shape[0]
+    r = here_ref.shape[1]
+    at = at_ref[0]
+
+    def place(mine, p_ref, q_ref):
+        one_hot = lax.broadcasted_iota(jnp.int32, (n_rows, r), 1) == (
+            at * n_rows + lax.broadcasted_iota(jnp.int32, (n_rows, r), 0)
+        )
+        cols = mm(one_hot.astype(F32), p_ref[:n, :], 1, 1)
+        group = LANES // rank
+        size = group * n_rows
+        for i, k in enumerate(range(0, n, LANES)):
+            block = jnp.concatenate([cols[:, k:k + LANES]] * group, 0)
+            block = jnp.where(same_block(block.shape, n_rows, rank), block, 0.0)
+            cores_ref[i * size:(i + 1) * size, :] = mm(block, q_ref[k:k + LANES, :], 1, 0)
+        here, away = (out_ref, in_ref) if mine else (in_ref, out_ref)
+        here[...] = here_ref[...]
+        away[...] = got_ref[n:, :]
+
+    @pl.when(at % 2 == 0)
+    def _():
+        place(True, sent_ref, got_ref)
+
+    @pl.when(at % 2 == 1)
+    def _():
+        place(False, got_ref, sent_ref)
 
 
 def last_kernel(whole_ref, raw_ref, sent_ref, here_ref, x_ref, y_ref):
@@ -157,13 +212,14 @@
     sent_ref[n:, :] = basis[half:, :]
 
 
-def call_on_whole(kernel, outs, n, r, *args):
+def call(kernel, shapes, args, scratch=(), scalars=0):
     return pl.pallas_call(
         kernel,
-        out_shape=[jax.ShapeDtypeStruct((rows, r), F32) for rows in outs],
-        in_specs=[pl.BlockSpec(memory_space=pltpu.VMEM)] * len(args),
-        out_specs=[pl.BlockSpec(memory_space=pltpu.VMEM)] * len(outs),
-        scratch_shapes=[pltpu.VMEM((r, r), F32), pltpu.VMEM((n, r), F32)],
+        out_shape=[jax.ShapeDtypeStruct(shape, F32) for shape in shapes],
+        in_specs=[pl.BlockSpec(memory_space=pltpu.SMEM)] * scalars
+        + [pl.BlockSpec(memory_space=pltpu.VMEM)] * (len(args) - scalars),
+        out_specs=[pl.BlockSpec(memory_space=pltpu.VMEM)] * len(shapes),
+        scratch_shapes=[pltpu.VMEM(shape, F32) for shape in scratch],
         compiler_params=pltpu.CompilerParams(vmem_limit_bytes=VMEM_BYTES),
     )(*args)
 
@@ -187,11 +243,13 @@
     chips = n_feat // 2
     core = lax.axis_index("feat") % 2
     same_core = [[2 * i + c for i in range(chips)] for c in range(2)]
+    side = math.isqrt(chips)
+    along_x = [[(y * side + x) * 2 + c for x in range(side)] for y in range(side) for c in range(2)]
+    along_y = [[(y * side + x) * 2 + c for y in range(side)] for x in range(side) for c in range(2)]
     n_z = n_tenant // 2
     along_z = [[h * n_z + z for z in range(n_z)] for h in range(2)]
     swap_cores = [(i, i ^ 1) for i in range(n_feat)]
     swap_halves = [(i, (i + n_z) % n_tenant) for i in range(n_tenant)]
-    root = 1.0 / math.sqrt(PROJ_WIDTH)
     mine = tenants // chips
 
     def pick(for_out, for_in):
@@ -210,40 +268,41 @@
     w = jnp.concatenate([pick(w_out, w_in), got[:tenants * rank]], 1)
     basis = jnp.concatenate([pick(initial_output_basis, initial_input_basis), got[tenants * rank:]], 0)
 
-    partial = mm(w, basis, 1, 0).reshape(chips, mine * rank, r)
-    p = (scatter_sum(partial, "feat", same_core) * root).reshape(mine, rank, r)
-    other_gram = to_partner(bmm(p, p, 2, 2))
-    factor = gather(bmm(other_gram, p, 2, 1).reshape(mine * rank, r), "feat", same_core)
-    factor = factor.reshape(tenants * rank, r)
+    n = tenants * rank
+    own_rows = mine * rank
+
+    partial = mm(w, basis, 1, 0).reshape(chips, own_rows, r)
+    p, gram = call(
+        functools.partial(first_gram_kernel, rank),
+        [(own_rows, r), (own_rows, own_rows)],
+        [exchange(partial, "feat", same_core)],
+    )
+    copies = call(first_factor_kernel, [(chips, own_rows, r)], [p, to_partner(gram)])[0]
+    factor = exchange(copies, "feat", same_core).reshape(n, r)
+    part = call(first_update_kernel, [(2 * feats, r)], [w, factor])[0]
 
     for step in range(ITERS):
-        part = mm(w, factor, 0, 0)
         own = scatter_sum(part.reshape(n_z, 2 * feats // n_z, r), "tenant", along_z)
         own = own + lax.ppermute(own, "tenant", swap_halves)
         raw = gather(own, "tenant", along_z).reshape(2 * feats, r)
-        own = scatter_sum(project(w, raw, chips), "feat", same_core)
-        whole = gather(own, "feat", same_core)
-        n = tenants * rank
+        chunk = (chips, 2 * own_rows + 3 * LANES // chips, LANES)
+        own = scatter_sum(call(project_kernel, [chunk], [w, raw])[0], "feat", same_core)
+        whole = gather(gather(own, "feat", along_y), "feat", along_x).reshape(chunk)
+        scratch = [(r, r), (n, r)]
         if step < ITERS - 1:
-            p = call_on_whole(middle_kernel, [n], n, r, whole)[0].reshape(tenants, rank, r)
-            other_gram = to_partner(bmm(p, p, 2, 2))
-            factor = bmm(other_gram, p, 2, 1).reshape(n, r)
-    sent, here = call_on_whole(last_kernel, [n + feats, feats], n, r, whole, raw)
-    got = to_partner(sent)
-    p, other, away = sent[:n], got[:n], got[n:]
+            p, gram = call(
+                functools.partial(middle_kernel, rank), [(n, r), (rank, n)], [whole], scratch
+            )
+            part = call(update_kernel, [(2 * feats, r)], [to_partner(gram), p, w], [(n, r)])[0]
+    sent, here = call(last_kernel, [(n + feats, r), (feats, r)], [whole, raw], scratch)
     n_rows = r // n_feat
-    first = lax.axis_index("feat") * n_rows
-    one_hot = lax.broadcasted_iota(jnp.int32, (n_rows, r), 1) == (
-        first + lax.broadcasted_iota(jnp.int32, (n_rows, r), 0)
-    )
-    cols = mm(one_hot.astype(F32), pick(p, other), 1, 1)
-    shape = (tenants, n_rows, tenants * rank)
-    own_tenant = lax.broadcasted_iota(jnp.int32, shape, 2) // rank == lax.broadcasted_iota(
-        jnp.int32, shape, 0
-    )
-    blocks = jnp.where(own_tenant, cols[None], 0.0).reshape(tenants * n_rows, tenants * rank)
-    cores = mm(blocks, pick(other, p), 1, 0).reshape(tenants, n_rows, r)
-    return cores, pick(here, away), pick(away, here)
+    cores, out_basis, in_basis = call(
+        functools.partial(cores_kernel, rank, n_rows),
+        [(tenants * n_rows, r), (feats, r), (feats, r)],
+        [lax.axis_index("feat").reshape(1), sent, to_partner(sent), here],
+        scalars=1,
+    )
+    return cores.reshape(tenants, n_rows, r), out_basis, in_basis
 
 
 def solution(mesh):

time: 281 us -> 278 us (0.989)
  blocking collectives: 184 us -> 176 us
  Pallas kernels: 20.8 us -> 27.7 us
  matrix products: 7.18 us -> 0.98 us
  starting transfers between devices: 35.5 us -> 41.3 us
    all_to_all x9 -> x11, blocking collectives: 184 us -> 176 us  [exchange(): lax.all_to_all(chunks, axis, 0, 0, tiled=True, axis_index_groups=groups)]
    pallas_call x4 -> x9, Pallas kernels: 20.8 us -> 27.7 us  [call(): pl.pallas_call(kernel, out_shape=[jax.ShapeDtypeStruct(shape, F32) for sh...]
    ppermute x4, starting transfers between devices: 21.7 us -> 27.5 us  [to_partner(): return lax.ppermute(x, 'feat', swap_cores)]
    dot_general x5 -> x1, matrix products: 5.7 us -> 0.98 us  [mm(): lax.dot_general(a, b, (((ca,), (cb,)), ((), ())), precision=HIGH_PRECISIO...]
where the time goes in v5:
time: 278 us; the launch traced here: 277 us
  blocking collectives  176 us (63%)
  starting transfers between devices  41.3 us (15%)
  Pallas kernels  27.7 us (10%)
  waiting for transfers between devices  27.6 us (10%)
    all_to_all x11, blocking collectives, exchange(): lax.all_to_all(chunks, axis, 0, 0, tiled=True, axis_index_groups=groups)  176 us
    pallas_call x9, Pallas kernels, call(): pl.pallas_call(kernel, out_shape=[jax.ShapeDtypeStruct(shape, F32) for sh...  27.7 us
    ppermute x4, starting transfers between devices, to_partner(): return lax.ppermute(x, 'feat', swap_cores)  27.5 us
    all_to_all x1, waiting for transfers between devices, exchange(): lax.all_to_all(chunks, axis, 0, 0, tiled=True, axis_index_groups=groups)  14 us
    ppermute x2, starting transfers between devices, body(): own = own + lax.ppermute(own, 'tenant', swap_halves)  9.51 us
    ppermute x2, waiting for transfers between devices, body(): own = own + lax.ppermute(own, 'tenant', swap_halves)  8.34 us
  transfers between devices with their start and end apart: 7, of which 7 were waited for; matrix products, arithmetic and copies ran while one was open for 0% of the time, Pallas kernels for 0%

profile of v5, /device:TPU:1, one launch (start us, length us, event | category | flops | bytes accessed | tf_op | source)
XLA Modules:
  0.0 277.0 jit_solution(5441272010912481285)
XLA Ops:
  0.6 0.0 copy-start.2
  0.7 0.0 copy-start.3
  0.7 0.0 copy-start.1
  0.7 1.5 maximum_select_fusion
  2.2 0.0 copy-start
  2.2 8.9 %collective-permute-start = (f32[768,256]{1,0:T(8,128)S(1)}, f32[768,256]{1,0:T(8,128)S(1)}, u32[]{:S(2)}, u32[]{:S(2)}) collective-permute-start(f32[768,256]{1,0:T(8,128)S(1)} %maximum_select_fusion), channel_id=1, source_target_pairs={{0,1},{1,0},{2,3},{3,2},{4,5},{5,4},{6,7},{7,6},{8,9},{9,8},{10,11... | collective-permute-start | bytes 2359304 | tf_op jit(solution)/shard_map/ppermute | solution.py:259
  11.2 0.0 copy-done.2
  11.2 0.0 copy-done.3
  11.2 0.0 copy-done.1
  11.2 0.0 copy-done
  11.2 0.1 broadcast_select_fusion
  11.3 1.7 collective-permute-done
  13.1 1.0 fusion
  14.1 17.0 %all_to_all.60.parts_ref = f32[16,32,256]{2,1,0:T(8,128)S(1)} all-to-all(f32[16,32,256]{2,1,0:T(8,128)S(1)} %bitcast.24), channel_id=1, replica_groups={{0,2,4,6,8,10,12,14,16,18,20,22,24,26,28,30},{1,3,5,7,9,11,13,15,17,19,..., dimensions={0} | all-to-all | bytes 1048576 | tf_op jit(solution)/shard_map/all_to_all | solution.py:228
  31.1 0.2 shard_map.67
  31.3 3.7 %collective-permute-start.1 = (f32[32,32]{1,0:T(8,128)S(1)}, f32[32,32]{1,0:T(8,128)S(1)}, u32[]{:S(2)}, u32[]{:S(2)}) collective-permute-start(f32[32,32]{1,0:T(8,128)S(1)} %get-tuple-element.13), channel_id=1, source_target_pairs={{0,1},{1,0},{2,3},{3,2},{4,5},{5,4},{6,7},{7,6},{8,9},{9,8},{10,11... | collective-permute-start | bytes 12296 | tf_op jit(solution)/shard_map/ppermute | solution.py:259
  35.0 0.8 collective-permute-done.1.gram_ref
  35.8 1.0 shard_map.68
  36.8 4.3 %all-to-all-start.1 = ((f32[16,32,256]{2,1,0:T(8,128)}), f32[16,32,256]{2,1,0:T(8,128)S(1)}, u32[]{:S(2)}, u32[]{:S(2)}) async-start(f32[16,32,256]{2,1,0:T(8,128)} %shard_map.68), calls=%async_computation.1 | async-start | bytes 1048576 | tf_op jit(solution)/shard_map/all_to_all | solution.py:228
  41.2 0.1 pad_maximum_fusion.w_ref
  41.3 14.0 %all-to-all-done.1 = f32[16,32,256]{2,1,0:T(8,128)S(1)} async-done(((f32[16,32,256]{2,1,0:T(8,128)}), f32[16,32,256]{2,1,0:T(8,128)S(1)}, u32[]{:S(2)}, u32[]{:S(2)}) %all-to-all-start.1) | async-done | bytes 524320 | tf_op jit(solution)/shard_map/all_to_all | solution.py:228
  55.3 1.2 shard_map.69
  56.6 23.3 %all_to_all.61 = f32[8,64,256]{2,1,0:T(8,128)S(1)} all-to-all(f32[8,64,256]{2,1,0:T(8,128)S(1)} %bitcast.20), channel_id=1, replica_groups={{0,32,64,96,128,160,192,224},{256,288,320,352,384,416,448,480},{1,33,65..., dimensions={0} | all-to-all | bytes 1048576 | tf_op jit(solution)/shard_map/all_to_all | solution.py:228
  79.9 4.8 %collective-permute-start.2 = (f32[64,256]{1,0:T(8,128)S(1)}, f32[64,256]{1,0:T(8,128)S(1)}, u32[]{:S(2)}, u32[]{:S(2)}) collective-permute-start(f32[64,256]{1,0:T(8,128)S(1)} %reduce_sum.36), channel_id=1, source_target_pairs={{0,256},{32,288},{64,320},{96,352},{128,384},{160,416},{192,448},{... | collective-permute-start | bytes 196616 | tf_op jit(solution)/shard_map/ppermute | solution.py:286
  84.6 4.2 %collective-permute-done.2 = f32[64,256]{1,0:T(8,128)S(1)} collective-permute-done((f32[64,256]{1,0:T(8,128)S(1)}, f32[64,256]{1,0:T(8,128)S(1)}, u32[]{:S(2)}, u32[]{:S(2)}) %collective-permute-start.2) | collective-permute-done | bytes 65568 | tf_op jit(solution)/shard_map/ppermute | solution.py:286
  88.9 15.6 %all_to_all.62 = f32[8,64,256]{2,1,0:T(8,128)S(1)} all-to-all(f32[8,64,256]{2,1,0:T(8,128)S(1)} %broadcast_in_dim.12), channel_id=1, replica_groups={{0,32,64,96,128,160,192,224},{256,288,320,352,384,416,448,480},{1,33,65..., dimensions={0} | all-to-all | bytes 1048576 | tf_op jit(solution)/shard_map/all_to_all | solution.py:228
  104.5 1.4 shard_map.70
  105.9 21.8 %all_to_all.63 = f32[16,88,128]{2,1,0:T(8,128)S(1)} all-to-all(f32[16,88,128]{2,1,0:T(8,128)S(1)} %shard_map.70), channel_id=1, replica_groups={{0,2,4,6,8,10,12,14,16,18,20,22,24,26,28,30},{1,3,5,7,9,11,13,15,17,19,..., dimensions={0} | all-to-all | bytes 1441792 | tf_op jit(solution)/shard_map/all_to_all | solution.py:228
  127.8 10.0 %all_to_all.64 = f32[4,88,128]{2,1,0:T(8,128)S(1)} all-to-all(f32[4,88,128]{2,1,0:T(8,128)S(1)} %broadcast_in_dim.13), channel_id=1, replica_groups={{0,8,16,24},{1,9,17,25},{2,10,18,26},{3,11,19,27},{4,12,20,28},{5,13,21..., dimensions={0} | all-to-all | bytes 360448 | tf_op jit(solution)/shard_map/all_to_all | solution.py:228
  137.8 10.5 %all_to_all.65 = f32[4,4,88,128]{3,2,1,0:T(8,128)S(1)} all-to-all(f32[4,4,88,128]{3,2,1,0:T(8,128)S(1)} %broadcast_in_dim.14), channel_id=1, replica_groups={{0,2,4,6},{1,3,5,7},{8,10,12,14},{9,11,13,15},{16,18,20,22},{17,19,21,2..., dimensions={0} | all-to-all | bytes 1441792 | tf_op jit(solution)/shard_map/all_to_all | solution.py:228
  148.3 9.9 %shard_map.71 = (f32[512,256]{1,0:T(8,128)S(1)}, f32[16,512]{1,0:T(8,128)S(1)}) custom-call(f32[16,88,128]{2,1,0:T(8,128)S(1)} %bitcast.17), custom_call_target="tpu_custom_call" | custom-call | tf_op jit(solution)/shard_map/pallas_call | solution.py:216
  158.3 7.9 %collective-permute-start.3 = (f32[16,512]{1,0:T(8,128)S(1)}, f32[16,512]{1,0:T(8,128)S(1)}, u32[]{:S(2)}, u32[]{:S(2)}) collective-permute-start(f32[16,512]{1,0:T(8,128)S(1)} %get-tuple-element.14), channel_id=1, source_target_pairs={{0,1},{1,0},{2,3},{3,2},{4,5},{5,4},{6,7},{7,6},{8,9},{9,8},{10,11... | collective-permute-start | bytes 98312 | tf_op jit(solution)/shard_map/ppermute | solution.py:259
  166.2 0.8 collective-permute-done.3.gram_ref
  167.0 1.6 shard_map.72
  168.6 20.6 %all_to_all.66 = f32[8,64,256]{2,1,0:T(8,128)S(1)} all-to-all(f32[8,64,256]{2,1,0:T(8,128)S(1)} %bitcast.19), channel_id=1, replica_groups={{0,32,64,96,128,160,192,224},{256,288,320,352,384,416,448,480},{1,33,65..., dimensions={0} | all-to-all | bytes 1048576 | tf_op jit(solution)/shard_map/all_to_all | solution.py:228
  189.3 4.8 %collective-permute-start.4 = (f32[64,256]{1,0:T(8,128)S(1)}, f32[64,256]{1,0:T(8,128)S(1)}, u32[]{:S(2)}, u32[]{:S(2)}) collective-permute-start(f32[64,256]{1,0:T(8,128)S(1)} %reduce_sum.38), channel_id=1, source_target_pairs={{0,256},{32,288},{64,320},{96,352},{128,384},{160,416},{192,448},{... | collective-permute-start | bytes 196616 | tf_op jit(solution)/shard_map/ppermute | solution.py:286
  194.1 4.2 %collective-permute-done.4 = f32[64,256]{1,0:T(8,128)S(1)} collective-permute-done((f32[64,256]{1,0:T(8,128)S(1)}, f32[64,256]{1,0:T(8,128)S(1)}, u32[]{:S(2)}, u32[]{:S(2)}) %collective-permute-start.4) | collective-permute-done | bytes 65568 | tf_op jit(solution)/shard_map/ppermute | solution.py:286
  198.3 16.7 %all_to_all.67 = f32[8,64,256]{2,1,0:T(8,128)S(1)} all-to-all(f32[8,64,256]{2,1,0:T(8,128)S(1)} %broadcast_in_dim.15), channel_id=1, replica_groups={{0,32,64,96,128,160,192,224},{256,288,320,352,384,416,448,480},{1,33,65..., dimensions={0} | all-to-all | bytes 1048576 | tf_op jit(solution)/shard_map/all_to_all | solution.py:228
  215.1 1.4 shard_map.73
  216.5 20.6 %all_to_all.68 = f32[16,88,128]{2,1,0:T(8,128)S(1)} all-to-all(f32[16,88,128]{2,1,0:T(8,128)S(1)} %shard_map.73), channel_id=1, replica_groups={{0,2,4,6,8,10,12,14,16,18,20,22,24,26,28,30},{1,3,5,7,9,11,13,15,17,19,..., dimensions={0} | all-to-all | bytes 1441792 | tf_op jit(solution)/shard_map/all_to_all | solution.py:228
  237.2 9.5 %all_to_all.69 = f32[4,88,128]{2,1,0:T(8,128)S(1)} all-to-all(f32[4,88,128]{2,1,0:T(8,128)S(1)} %broadcast_in_dim.16), channel_id=1, replica_groups={{0,8,16,24},{1,9,17,25},{2,10,18,26},{3,11,19,27},{4,12,20,28},{5,13,21..., dimensions={0} | all-to-all | bytes 360448 | tf_op jit(solution)/shard_map/all_to_all | solution.py:228
  246.7 10.5 %all_to_all.70 = f32[4,4,88,128]{3,2,1,0:T(8,128)S(1)} all-to-all(f32[4,4,88,128]{3,2,1,0:T(8,128)S(1)} %broadcast_in_dim.17), channel_id=1, replica_groups={{0,2,4,6},{1,3,5,7},{8,10,12,14},{9,11,13,15},{16,18,20,22},{17,19,21,2..., dimensions={0} | all-to-all | bytes 1441792 | tf_op jit(solution)/shard_map/all_to_all | solution.py:228
  257.2 9.2 %shard_map.74 = (f32[768,256]{1,0:T(8,128)S(1)}, f32[256,256]{1,0:T(8,128)S(1)}) custom-call(f32[16,88,128]{2,1,0:T(8,128)S(1)} %bitcast.16, f32[512,256]{1,0:T(8,128)S(1)} %bitcast.15), custom_call_target="tpu_custom_call" | custom-call | tf_op jit(solution)/shard_map/pallas_call | solution.py:216
  266.4 6.9 %collective-permute-start.5 = (f32[768,256]{1,0:T(8,128)S(1)}, f32[768,256]{1,0:T(8,128)S(1)}, u32[]{:S(2)}, u32[]{:S(2)}) collective-permute-start(f32[768,256]{1,0:T(8,128)S(1)} %get-tuple-element.16.sent_ref), channel_id=1, source_target_pairs={{0,1},{1,0},{2,3},{3,2},{4,5},{5,4},{6,7},{7,6},{8,9},{9,8},{10,11... | collective-permute-start | bytes 2359304 | tf_op jit(solution)/shard_map/ppermute | solution.py:259
  273.3 1.9 collective-permute-done.5.got_ref
  275.2 1.8 shard_map.75
  (15 shorter events, 0.5 us)
Async XLA Ops:
  0.6 10.5 %copy-start.2 = (f32[256,256]{1,0:T(8,128)S(1)}, f32[256,256]{1,0:T(8,128)}, u32[]{:S(2)}) copy-start(f32[256,256]{1,0:T(8,128)} %param.7) | copy-start | bytes 786436
  0.7 10.5 %copy-start.3 = (f32[256,256]{1,0:T(8,128)S(1)}, f32[256,256]{1,0:T(8,128)}, u32[]{:S(2)}) copy-start(f32[256,256]{1,0:T(8,128)} %param.6) | copy-start | bytes 786436
  0.7 10.6 %copy-start.1 = (f32[32,16,256]{2,1,0:T(8,128)S(1)}, f32[32,16,256]{2,1,0:T(8,128)}, u32[]{:S(2)}) copy-start(f32[32,16,256]{2,1,0:T(8,128)} %param.5) | copy-start | bytes 1572868
  2.2 9.0 %copy-start = (f32[32,16,256]{2,1,0:T(8,128)S(1)}, f32[32,16,256]{2,1,0:T(8,128)}, u32[]{:S(2)}) copy-start(f32[32,16,256]{2,1,0:T(8,128)} %param.4) | copy-start | bytes 1572868
  2.2 10.8 %collective-permute-start = (f32[768,256]{1,0:T(8,128)S(1)}, f32[768,256]{1,0:T(8,128)S(1)}, u32[]{:S(2)}, u32[]{:S(2)}) collective-permute-start(f32[768,256]{1,0:T(8,128)S(1)} %maximum_select_fusion), channel_id=1, source_target_pairs={{0,1},{1,0},{2,3},{3,2},{4,5},{5,4},{6,7},{7,6},{8,9},{9,8},{10,11... | collective-permute-start | bytes 2359304 | tf_op jit(solution)/shard_map/ppermute | solution.py:259
  31.3 4.6 %collective-permute-start.1 = (f32[32,32]{1,0:T(8,128)S(1)}, f32[32,32]{1,0:T(8,128)S(1)}, u32[]{:S(2)}, u32[]{:S(2)}) collective-permute-start(f32[32,32]{1,0:T(8,128)S(1)} %get-tuple-element.13), channel_id=1, source_target_pairs={{0,1},{1,0},{2,3},{3,2},{4,5},{5,4},{6,7},{7,6},{8,9},{9,8},{10,11... | collective-permute-start | bytes 12296 | tf_op jit(solution)/shard_map/ppermute | solution.py:259
  36.8 18.5 %all-to-all-start.1 = ((f32[16,32,256]{2,1,0:T(8,128)}), f32[16,32,256]{2,1,0:T(8,128)S(1)}, u32[]{:S(2)}, u32[]{:S(2)}) async-start(f32[16,32,256]{2,1,0:T(8,128)} %shard_map.68), calls=%async_computation.1 | async-start | bytes 1048576 | tf_op jit(solution)/shard_map/all_to_all | solution.py:228
  79.9 8.9 %collective-permute-start.2 = (f32[64,256]{1,0:T(8,128)S(1)}, f32[64,256]{1,0:T(8,128)S(1)}, u32[]{:S(2)}, u32[]{:S(2)}) collective-permute-start(f32[64,256]{1,0:T(8,128)S(1)} %reduce_sum.36), channel_id=1, source_target_pairs={{0,256},{32,288},{64,320},{96,352},{128,384},{160,416},{192,448},{... | collective-permute-start | bytes 196616 | tf_op jit(solution)/shard_map/ppermute | solution.py:286
  158.3 8.8 %collective-permute-start.3 = (f32[16,512]{1,0:T(8,128)S(1)}, f32[16,512]{1,0:T(8,128)S(1)}, u32[]{:S(2)}, u32[]{:S(2)}) collective-permute-start(f32[16,512]{1,0:T(8,128)S(1)} %get-tuple-element.14), channel_id=1, source_target_pairs={{0,1},{1,0},{2,3},{3,2},{4,5},{5,4},{6,7},{7,6},{8,9},{9,8},{10,11... | collective-permute-start | bytes 98312 | tf_op jit(solution)/shard_map/ppermute | solution.py:259
  189.3 8.9 %collective-permute-start.4 = (f32[64,256]{1,0:T(8,128)S(1)}, f32[64,256]{1,0:T(8,128)S(1)}, u32[]{:S(2)}, u32[]{:S(2)}) collective-permute-start(f32[64,256]{1,0:T(8,128)S(1)} %reduce_sum.38), channel_id=1, source_target_pairs={{0,256},{32,288},{64,320},{96,352},{128,384},{160,416},{192,448},{... | collective-permute-start | bytes 196616 | tf_op jit(solution)/shard_map/ppermute | solution.py:286
  266.4 8.8 %collective-permute-start.5 = (f32[768,256]{1,0:T(8,128)S(1)}, f32[768,256]{1,0:T(8,128)S(1)}, u32[]{:S(2)}, u32[]{:S(2)}) collective-permute-start(f32[768,256]{1,0:T(8,128)S(1)} %get-tuple-element.16.sent_ref), channel_id=1, source_target_pairs={{0,1},{1,0},{2,3},{3,2},{4,5},{5,4},{6,7},{7,6},{8,9},{9,8},{10,11... | collective-permute-start | bytes 2359304 | tf_op jit(solution)/shard_map/ppermute | solution.py:259

commit v6 on v5

--- a/solution.py
+++ b/solution.py
@@ -212,10 +212,10 @@
     sent_ref[n:, :] = basis[half:, :]
 
 
-def call(kernel, shapes, args, scratch=(), scalars=0):
+def call(kernel, shapes, args, scratch=(), scalars=0, out=jax.ShapeDtypeStruct):
     return pl.pallas_call(
         kernel,
-        out_shape=[jax.ShapeDtypeStruct(shape, F32) for shape in shapes],
+        out_shape=[out(shape, F32) for shape in shapes],
         in_specs=[pl.BlockSpec(memory_space=pltpu.SMEM)] * scalars
         + [pl.BlockSpec(memory_space=pltpu.VMEM)] * (len(args) - scalars),
         out_specs=[pl.BlockSpec(memory_space=pltpu.VMEM)] * len(shapes),
@@ -277,7 +277,9 @@
         [(own_rows, r), (own_rows, own_rows)],
         [exchange(partial, "feat", same_core)],
     )
-    copies = call(first_factor_kernel, [(chips, own_rows, r)], [p, to_partner(gram)])[0]
+    copies = call(
+        first_factor_kernel, [(chips, own_rows, r)], [p, to_partner(gram)], out=pltpu.VMEM
+    )[0]
     factor = exchange(copies, "feat", same_core).reshape(n, r)
     part = call(first_update_kernel, [(2 * feats, r)], [w, factor])[0]
 

time: 278 us -> 278 us (level)
  no operation moved by 1% of the time
where the time goes in v6:
time: 278 us; the launch traced here: 277 us
  blocking collectives  176 us (63%)
  starting transfers between devices  41.3 us (15%)
  Pallas kernels  27.7 us (10%)
  waiting for transfers between devices  27.6 us (10%)
    all_to_all x11, blocking collectives, exchange(): lax.all_to_all(chunks, axis, 0, 0, tiled=True, axis_index_groups=groups)  176 us
    pallas_call x9, Pallas kernels, call(): pl.pallas_call(kernel, out_shape=[out(shape, F32) for shape in shapes], i...  27.7 us
    ppermute x4, starting transfers between devices, to_partner(): return lax.ppermute(x, 'feat', swap_cores)  27.5 us
    all_to_all x1, waiting for transfers between devices, exchange(): lax.all_to_all(chunks, axis, 0, 0, tiled=True, axis_index_groups=groups)  14 us
    ppermute x2, starting transfers between devices, body(): own = own + lax.ppermute(own, 'tenant', swap_halves)  9.51 us
    ppermute x2, waiting for transfers between devices, body(): own = own + lax.ppermute(own, 'tenant', swap_halves)  8.34 us
  transfers between devices with their start and end apart: 7, of which 7 were waited for; matrix products, arithmetic and copies ran while one was open for 0% of the time, Pallas kernels for 0%

profile of v6, /device:TPU:1, one launch (start us, length us, event | category | flops | bytes accessed | tf_op | source)
XLA Modules:
  0.0 277.0 jit_solution(5441272010912481285)
XLA Ops:
  0.6 0.0 copy-start.2
  0.7 0.0 copy-start.3
  0.7 0.0 copy-start.1
  0.7 1.5 maximum_select_fusion
  2.2 0.0 copy-start
  2.2 8.9 %collective-permute-start = (f32[768,256]{1,0:T(8,128)S(1)}, f32[768,256]{1,0:T(8,128)S(1)}, u32[]{:S(2)}, u32[]{:S(2)}) collective-permute-start(f32[768,256]{1,0:T(8,128)S(1)} %maximum_select_fusion), channel_id=1, source_target_pairs={{0,1},{1,0},{2,3},{3,2},{4,5},{5,4},{6,7},{7,6},{8,9},{9,8},{10,11... | collective-permute-start | bytes 2359304 | tf_op jit(solution)/shard_map/ppermute | solution.py:259
  11.2 0.0 copy-done.2
  11.2 0.0 copy-done.3
  11.2 0.0 copy-done.1
  11.2 0.0 copy-done
  11.2 0.1 broadcast_select_fusion
  11.3 1.7 collective-permute-done
  13.1 1.0 fusion
  14.1 17.0 %all_to_all.60.parts_ref = f32[16,32,256]{2,1,0:T(8,128)S(1)} all-to-all(f32[16,32,256]{2,1,0:T(8,128)S(1)} %bitcast.24), channel_id=1, replica_groups={{0,2,4,6,8,10,12,14,16,18,20,22,24,26,28,30},{1,3,5,7,9,11,13,15,17,19,..., dimensions={0} | all-to-all | bytes 1048576 | tf_op jit(solution)/shard_map/all_to_all | solution.py:228
  31.1 0.2 shard_map.67
  31.3 3.7 %collective-permute-start.1 = (f32[32,32]{1,0:T(8,128)S(1)}, f32[32,32]{1,0:T(8,128)S(1)}, u32[]{:S(2)}, u32[]{:S(2)}) collective-permute-start(f32[32,32]{1,0:T(8,128)S(1)} %get-tuple-element.13), channel_id=1, source_target_pairs={{0,1},{1,0},{2,3},{3,2},{4,5},{5,4},{6,7},{7,6},{8,9},{9,8},{10,11... | collective-permute-start | bytes 12296 | tf_op jit(solution)/shard_map/ppermute | solution.py:259
  35.0 0.8 collective-permute-done.1.gram_ref
  35.8 1.0 shard_map.68
  36.8 4.3 %all-to-all-start.1 = ((f32[16,32,256]{2,1,0:T(8,128)}), f32[16,32,256]{2,1,0:T(8,128)S(1)}, u32[]{:S(2)}, u32[]{:S(2)}) async-start(f32[16,32,256]{2,1,0:T(8,128)} %shard_map.68), calls=%async_computation.1 | async-start | bytes 1048576 | tf_op jit(solution)/shard_map/all_to_all | solution.py:228
  41.2 0.1 pad_maximum_fusion.w_ref
  41.3 14.0 %all-to-all-done.1 = f32[16,32,256]{2,1,0:T(8,128)S(1)} async-done(((f32[16,32,256]{2,1,0:T(8,128)}), f32[16,32,256]{2,1,0:T(8,128)S(1)}, u32[]{:S(2)}, u32[]{:S(2)}) %all-to-all-start.1) | async-done | bytes 524320 | tf_op jit(solution)/shard_map/all_to_all | solution.py:228
  55.3 1.2 shard_map.69
  56.6 23.3 %all_to_all.61 = f32[8,64,256]{2,1,0:T(8,128)S(1)} all-to-all(f32[8,64,256]{2,1,0:T(8,128)S(1)} %bitcast.20), channel_id=1, replica_groups={{0,32,64,96,128,160,192,224},{256,288,320,352,384,416,448,480},{1,33,65..., dimensions={0} | all-to-all | bytes 1048576 | tf_op jit(solution)/shard_map/all_to_all | solution.py:228
  79.9 4.8 %collective-permute-start.2 = (f32[64,256]{1,0:T(8,128)S(1)}, f32[64,256]{1,0:T(8,128)S(1)}, u32[]{:S(2)}, u32[]{:S(2)}) collective-permute-start(f32[64,256]{1,0:T(8,128)S(1)} %reduce_sum.36), channel_id=1, source_target_pairs={{0,256},{32,288},{64,320},{96,352},{128,384},{160,416},{192,448},{... | collective-permute-start | bytes 196616 | tf_op jit(solution)/shard_map/ppermute | solution.py:288
  84.6 4.2 %collective-permute-done.2 = f32[64,256]{1,0:T(8,128)S(1)} collective-permute-done((f32[64,256]{1,0:T(8,128)S(1)}, f32[64,256]{1,0:T(8,128)S(1)}, u32[]{:S(2)}, u32[]{:S(2)}) %collective-permute-start.2) | collective-permute-done | bytes 65568 | tf_op jit(solution)/shard_map/ppermute | solution.py:288
  88.9 15.6 %all_to_all.62 = f32[8,64,256]{2,1,0:T(8,128)S(1)} all-to-all(f32[8,64,256]{2,1,0:T(8,128)S(1)} %broadcast_in_dim.12), channel_id=1, replica_groups={{0,32,64,96,128,160,192,224},{256,288,320,352,384,416,448,480},{1,33,65..., dimensions={0} | all-to-all | bytes 1048576 | tf_op jit(solution)/shard_map/all_to_all | solution.py:228
  104.5 1.4 shard_map.70
  105.9 21.8 %all_to_all.63 = f32[16,88,128]{2,1,0:T(8,128)S(1)} all-to-all(f32[16,88,128]{2,1,0:T(8,128)S(1)} %shard_map.70), channel_id=1, replica_groups={{0,2,4,6,8,10,12,14,16,18,20,22,24,26,28,30},{1,3,5,7,9,11,13,15,17,19,..., dimensions={0} | all-to-all | bytes 1441792 | tf_op jit(solution)/shard_map/all_to_all | solution.py:228
  127.8 10.0 %all_to_all.64 = f32[4,88,128]{2,1,0:T(8,128)S(1)} all-to-all(f32[4,88,128]{2,1,0:T(8,128)S(1)} %broadcast_in_dim.13), channel_id=1, replica_groups={{0,8,16,24},{1,9,17,25},{2,10,18,26},{3,11,19,27},{4,12,20,28},{5,13,21..., dimensions={0} | all-to-all | bytes 360448 | tf_op jit(solution)/shard_map/all_to_all | solution.py:228
  137.8 10.5 %all_to_all.65 = f32[4,4,88,128]{3,2,1,0:T(8,128)S(1)} all-to-all(f32[4,4,88,128]{3,2,1,0:T(8,128)S(1)} %broadcast_in_dim.14), channel_id=1, replica_groups={{0,2,4,6},{1,3,5,7},{8,10,12,14},{9,11,13,15},{16,18,20,22},{17,19,21,2..., dimensions={0} | all-to-all | bytes 1441792 | tf_op jit(solution)/shard_map/all_to_all | solution.py:228
  148.3 9.9 %shard_map.71 = (f32[512,256]{1,0:T(8,128)S(1)}, f32[16,512]{1,0:T(8,128)S(1)}) custom-call(f32[16,88,128]{2,1,0:T(8,128)S(1)} %bitcast.17), custom_call_target="tpu_custom_call" | custom-call | tf_op jit(solution)/shard_map/pallas_call | solution.py:216
  158.3 7.9 %collective-permute-start.3 = (f32[16,512]{1,0:T(8,128)S(1)}, f32[16,512]{1,0:T(8,128)S(1)}, u32[]{:S(2)}, u32[]{:S(2)}) collective-permute-start(f32[16,512]{1,0:T(8,128)S(1)} %get-tuple-element.14), channel_id=1, source_target_pairs={{0,1},{1,0},{2,3},{3,2},{4,5},{5,4},{6,7},{7,6},{8,9},{9,8},{10,11... | collective-permute-start | bytes 98312 | tf_op jit(solution)/shard_map/ppermute | solution.py:259
  166.2 0.8 collective-permute-done.3.gram_ref
  167.0 1.6 shard_map.72
  168.6 20.6 %all_to_all.66 = f32[8,64,256]{2,1,0:T(8,128)S(1)} all-to-all(f32[8,64,256]{2,1,0:T(8,128)S(1)} %bitcast.19), channel_id=1, replica_groups={{0,32,64,96,128,160,192,224},{256,288,320,352,384,416,448,480},{1,33,65..., dimensions={0} | all-to-all | bytes 1048576 | tf_op jit(solution)/shard_map/all_to_all | solution.py:228
  189.3 4.8 %collective-permute-start.4 = (f32[64,256]{1,0:T(8,128)S(1)}, f32[64,256]{1,0:T(8,128)S(1)}, u32[]{:S(2)}, u32[]{:S(2)}) collective-permute-start(f32[64,256]{1,0:T(8,128)S(1)} %reduce_sum.38), channel_id=1, source_target_pairs={{0,256},{32,288},{64,320},{96,352},{128,384},{160,416},{192,448},{... | collective-permute-start | bytes 196616 | tf_op jit(solution)/shard_map/ppermute | solution.py:288
  194.1 4.2 %collective-permute-done.4 = f32[64,256]{1,0:T(8,128)S(1)} collective-permute-done((f32[64,256]{1,0:T(8,128)S(1)}, f32[64,256]{1,0:T(8,128)S(1)}, u32[]{:S(2)}, u32[]{:S(2)}) %collective-permute-start.4) | collective-permute-done | bytes 65568 | tf_op jit(solution)/shard_map/ppermute | solution.py:288
  198.3 16.7 %all_to_all.67 = f32[8,64,256]{2,1,0:T(8,128)S(1)} all-to-all(f32[8,64,256]{2,1,0:T(8,128)S(1)} %broadcast_in_dim.15), channel_id=1, replica_groups={{0,32,64,96,128,160,192,224},{256,288,320,352,384,416,448,480},{1,33,65..., dimensions={0} | all-to-all | bytes 1048576 | tf_op jit(solution)/shard_map/all_to_all | solution.py:228
  215.1 1.4 shard_map.73
  216.5 20.6 %all_to_all.68 = f32[16,88,128]{2,1,0:T(8,128)S(1)} all-to-all(f32[16,88,128]{2,1,0:T(8,128)S(1)} %shard_map.73), channel_id=1, replica_groups={{0,2,4,6,8,10,12,14,16,18,20,22,24,26,28,30},{1,3,5,7,9,11,13,15,17,19,..., dimensions={0} | all-to-all | bytes 1441792 | tf_op jit(solution)/shard_map/all_to_all | solution.py:228
  237.2 9.5 %all_to_all.69 = f32[4,88,128]{2,1,0:T(8,128)S(1)} all-to-all(f32[4,88,128]{2,1,0:T(8,128)S(1)} %broadcast_in_dim.16), channel_id=1, replica_groups={{0,8,16,24},{1,9,17,25},{2,10,18,26},{3,11,19,27},{4,12,20,28},{5,13,21..., dimensions={0} | all-to-all | bytes 360448 | tf_op jit(solution)/shard_map/all_to_all | solution.py:228
  246.7 10.5 %all_to_all.70 = f32[4,4,88,128]{3,2,1,0:T(8,128)S(1)} all-to-all(f32[4,4,88,128]{3,2,1,0:T(8,128)S(1)} %broadcast_in_dim.17), channel_id=1, replica_groups={{0,2,4,6},{1,3,5,7},{8,10,12,14},{9,11,13,15},{16,18,20,22},{17,19,21,2..., dimensions={0} | all-to-all | bytes 1441792 | tf_op jit(solution)/shard_map/all_to_all | solution.py:228
  257.2 9.2 %shard_map.74 = (f32[768,256]{1,0:T(8,128)S(1)}, f32[256,256]{1,0:T(8,128)S(1)}) custom-call(f32[16,88,128]{2,1,0:T(8,128)S(1)} %bitcast.16, f32[512,256]{1,0:T(8,128)S(1)} %bitcast.15), custom_call_target="tpu_custom_call" | custom-call | tf_op jit(solution)/shard_map/pallas_call | solution.py:216
  266.4 6.9 %collective-permute-start.5 = (f32[768,256]{1,0:T(8,128)S(1)}, f32[768,256]{1,0:T(8,128)S(1)}, u32[]{:S(2)}, u32[]{:S(2)}) collective-permute-start(f32[768,256]{1,0:T(8,128)S(1)} %get-tuple-element.16.sent_ref), channel_id=1, source_target_pairs={{0,1},{1,0},{2,3},{3,2},{4,5},{5,4},{6,7},{7,6},{8,9},{9,8},{10,11... | collective-permute-start | bytes 2359304 | tf_op jit(solution)/shard_map/ppermute | solution.py:259
  273.3 1.9 collective-permute-done.5.got_ref
  275.2 1.8 shard_map.75
  (15 shorter events, 0.5 us)
Async XLA Ops:
  0.6 10.5 %copy-start.2 = (f32[256,256]{1,0:T(8,128)S(1)}, f32[256,256]{1,0:T(8,128)}, u32[]{:S(2)}) copy-start(f32[256,256]{1,0:T(8,128)} %param.7) | copy-start | bytes 786436
  0.7 10.5 %copy-start.3 = (f32[256,256]{1,0:T(8,128)S(1)}, f32[256,256]{1,0:T(8,128)}, u32[]{:S(2)}) copy-start(f32[256,256]{1,0:T(8,128)} %param.6) | copy-start | bytes 786436
  0.7 10.6 %copy-start.1 = (f32[32,16,256]{2,1,0:T(8,128)S(1)}, f32[32,16,256]{2,1,0:T(8,128)}, u32[]{:S(2)}) copy-start(f32[32,16,256]{2,1,0:T(8,128)} %param.5) | copy-start | bytes 1572868
  2.2 9.0 %copy-start = (f32[32,16,256]{2,1,0:T(8,128)S(1)}, f32[32,16,256]{2,1,0:T(8,128)}, u32[]{:S(2)}) copy-start(f32[32,16,256]{2,1,0:T(8,128)} %param.4) | copy-start | bytes 1572868
  2.2 10.8 %collective-permute-start = (f32[768,256]{1,0:T(8,128)S(1)}, f32[768,256]{1,0:T(8,128)S(1)}, u32[]{:S(2)}, u32[]{:S(2)}) collective-permute-start(f32[768,256]{1,0:T(8,128)S(1)} %maximum_select_fusion), channel_id=1, source_target_pairs={{0,1},{1,0},{2,3},{3,2},{4,5},{5,4},{6,7},{7,6},{8,9},{9,8},{10,11... | collective-permute-start | bytes 2359304 | tf_op jit(solution)/shard_map/ppermute | solution.py:259
  31.3 4.6 %collective-permute-start.1 = (f32[32,32]{1,0:T(8,128)S(1)}, f32[32,32]{1,0:T(8,128)S(1)}, u32[]{:S(2)}, u32[]{:S(2)}) collective-permute-start(f32[32,32]{1,0:T(8,128)S(1)} %get-tuple-element.13), channel_id=1, source_target_pairs={{0,1},{1,0},{2,3},{3,2},{4,5},{5,4},{6,7},{7,6},{8,9},{9,8},{10,11... | collective-permute-start | bytes 12296 | tf_op jit(solution)/shard_map/ppermute | solution.py:259
  36.8 18.5 %all-to-all-start.1 = ((f32[16,32,256]{2,1,0:T(8,128)}), f32[16,32,256]{2,1,0:T(8,128)S(1)}, u32[]{:S(2)}, u32[]{:S(2)}) async-start(f32[16,32,256]{2,1,0:T(8,128)} %shard_map.68), calls=%async_computation.1 | async-start | bytes 1048576 | tf_op jit(solution)/shard_map/all_to_all | solution.py:228
  79.9 8.9 %collective-permute-start.2 = (f32[64,256]{1,0:T(8,128)S(1)}, f32[64,256]{1,0:T(8,128)S(1)}, u32[]{:S(2)}, u32[]{:S(2)}) collective-permute-start(f32[64,256]{1,0:T(8,128)S(1)} %reduce_sum.36), channel_id=1, source_target_pairs={{0,256},{32,288},{64,320},{96,352},{128,384},{160,416},{192,448},{... | collective-permute-start | bytes 196616 | tf_op jit(solution)/shard_map/ppermute | solution.py:288
  158.3 8.8 %collective-permute-start.3 = (f32[16,512]{1,0:T(8,128)S(1)}, f32[16,512]{1,0:T(8,128)S(1)}, u32[]{:S(2)}, u32[]{:S(2)}) collective-permute-start(f32[16,512]{1,0:T(8,128)S(1)} %get-tuple-element.14), channel_id=1, source_target_pairs={{0,1},{1,0},{2,3},{3,2},{4,5},{5,4},{6,7},{7,6},{8,9},{9,8},{10,11... | collective-permute-start | bytes 98312 | tf_op jit(solution)/shard_map/ppermute | solution.py:259
  189.3 8.9 %collective-permute-start.4 = (f32[64,256]{1,0:T(8,128)S(1)}, f32[64,256]{1,0:T(8,128)S(1)}, u32[]{:S(2)}, u32[]{:S(2)}) collective-permute-start(f32[64,256]{1,0:T(8,128)S(1)} %reduce_sum.38), channel_id=1, source_target_pairs={{0,256},{32,288},{64,320},{96,352},{128,384},{160,416},{192,448},{... | collective-permute-start | bytes 196616 | tf_op jit(solution)/shard_map/ppermute | solution.py:288
  266.4 8.8 %collective-permute-start.5 = (f32[768,256]{1,0:T(8,128)S(1)}, f32[768,256]{1,0:T(8,128)S(1)}, u32[]{:S(2)}, u32[]{:S(2)}) collective-permute-start(f32[768,256]{1,0:T(8,128)S(1)} %get-tuple-element.16.sent_ref), channel_id=1, source_target_pairs={{0,1},{1,0},{2,3},{3,2},{4,5},{5,4},{6,7},{7,6},{8,9},{9,8},{10,11... | collective-permute-start | bytes 2359304 | tf_op jit(solution)/shard_map/ppermute | solution.py:259
